TPU v7x, 32 devices: a whole 2x2x4 slice. The times are simulated.
32 devices in a mesh: groups: 2 (over y), row: 4 (over z), col: 4 (over x, core).
Axes of the slice: x: 2, y: 2, z: 4, core: 2. Of those that a mesh axis runs over, the one named last changes fastest.
Arguments:
- pair: bfloat16 [512, 256, 128], P(('groups', 'row'), 'col'), parts along dimension 0, may hold values from -300 to 300
- single: bfloat16 [512, 384], P(('groups', 'row')), parts along dimension 0, may hold values from -6 to 6
- token_mask: int32 [512], P(('groups', 'col')), parts along dimension 0, may hold values from 0 to 1, as said below
- pair_gain: float32 [128], replicated, may hold values from 0.25 to 1.75
- transition_in: bfloat16 [128, 1024], replicated, may hold values from -0.5 to 0.5
- transition_out: bfloat16 [512, 128], replicated, may hold values from -0.25 to 0.25
- bias_weight: float32 [128, 16], replicated, may hold values from -0.9 to 0.9
- bin_weight: float32 [128, 64], replicated, may hold values from -0.5 to 0.5
- single_gain: float32 [384], replicated, may hold values from 0.25 to 1.75
- attention_in: bfloat16 [384, 1536], replicated, may hold values from -0.3125 to 0.3125
- attention_out: bfloat16 [384, 384], replicated, may hold values from -0.8984375 to 0.8984375
Outputs:
- distogram: float32 [512, 256, 64], P(('groups', 'row'), 'col'), parts along dimension 0
- single_update: bfloat16 [512, 384], P(('groups', 'row')), parts along dimension 0
There are 2 independent parts, one for each index of `groups`. A program takes and returns all parts, laid end to end along the dimension named above; an argument that names none is the same for every part. Nothing has to cross between parts.
Inputs may be any that keep to these rules, and one draw needn't show every extreme that they name: `token_mask`: 1 on a prefix of at least 128 tokens, 0 after it; at least the last token is 0.
All inputs are finite; a program needn't handle non-finite values.
Results may differ from a plain program's by a relative error of at most 0.014.
Values may be sent and summed in bfloat16 or wider, within the bound.
No kernel may reach another device: no remote copies, remote signals or barrier semaphores. Data moves between devices by JAX's collectives and lax.ppermute only.
A program may use at most 64 MiB of HBM per device.

v0:
```python
import math

import jax
import jax.numpy as jnp
from jax import lax
from jax.sharding import PartitionSpec as P


def from_root(value, axis, source):
    kept = jnp.where(lax.axis_index(axis) == source, value, 0).astype(value.dtype)
    return lax.psum(kept, axis)


def combined_all(value, axis, join):
    pieces = jax.tree.map(lambda part: lax.all_gather(part, axis), value)
    head = jax.tree.map(lambda part: part[0], pieces)
    tail = jax.tree.map(lambda part: part[1:], pieces)
    total, _ = lax.scan(lambda total, section: (join(total, section), None), head, tail)
    return total


def layer_norm(values, gain):
    average = jnp.mean(values, axis=-1, keepdims=True)
    centered = values - average
    variance = jnp.mean(centered * centered, axis=-1, keepdims=True)
    return centered * lax.rsqrt(variance + 1e-05) * gain


def rescale(summed, factor):
    rows_count, heads_count = factor.shape
    return (summed.reshape(rows_count, heads_count, -1) * factor[..., None]).reshape(rows_count, -1)


def combine_parts(earlier, later):
    first_top, first_total, first_sum = earlier
    second_top, second_total, second_sum = later
    joined_top = jnp.maximum(first_top, second_top)
    first_factor = jnp.exp(first_top - joined_top)
    second_factor = jnp.exp(second_top - joined_top)
    joined_total = first_total * first_factor + second_total * second_factor
    joined_sum = rescale(first_sum, first_factor) + rescale(second_sum, second_factor)
    return (joined_top, joined_total, joined_sum)


def body(
    pair,
    single,
    token_mask,
    pair_gain,
    transition_in,
    transition_out,
    bias_weight,
    bin_weight,
    single_gain,
    attention_in,
    attention_out,
):
    tile_rows, tile_cols, channels = pair.shape
    width = single.shape[1]
    heads_count = bias_weight.shape[1]
    head_width = width // heads_count
    hidden_units = transition_out.shape[0]
    bins_count = bin_weight.shape[1]
    flat = pair.reshape(tile_rows * tile_cols, channels).astype(jnp.float32)
    normed = layer_norm(flat, pair_gain).astype(jnp.bfloat16)
    both = jnp.dot(normed, transition_in, preferred_element_type=jnp.float32)
    gated_pair = (jax.nn.silu(both[:, :hidden_units]) * both[:, hidden_units:]).astype(jnp.bfloat16)
    updated = flat + jnp.dot(gated_pair, transition_out, preferred_element_type=jnp.float32)
    biases = jnp.dot(updated, bias_weight, precision=lax.Precision.HIGHEST).reshape(
        tile_rows, tile_cols, heads_count
    )
    halves = jnp.dot(updated, bin_weight, precision=lax.Precision.HIGHEST).reshape(
        tile_rows, tile_cols * bins_count
    )
    stacked = halves.reshape(1, tile_rows, tile_cols * bins_count)
    spread = lax.all_to_all(stacked, "col", split_axis=1, concat_axis=0, tiled=True)
    moving = lax.all_to_all(
        lax.all_to_all(spread, "row", split_axis=0, concat_axis=0, tiled=True),
        "col",
        split_axis=0,
        concat_axis=1,
        tiled=True,
    )
    mirrored = moving.reshape(tile_cols, tile_rows, bins_count).swapaxes(0, 1)
    symmetric = halves.reshape(tile_rows, tile_cols, bins_count) + mirrored
    distogram = jax.nn.softmax(symmetric, axis=-1)
    key_rows = from_root(single, "row", lax.axis_index("col"))
    query_normed = layer_norm(single.astype(jnp.float32), single_gain).astype(jnp.bfloat16)
    key_normed = layer_norm(key_rows.astype(jnp.float32), single_gain).astype(jnp.bfloat16)
    queries = jnp.dot(query_normed, attention_in[:, :width], preferred_element_type=jnp.float32)
    gates = jnp.dot(query_normed, attention_in[:, 3 * width :], preferred_element_type=jnp.float32)
    key_side = jnp.dot(
        key_normed, attention_in[:, width : 3 * width], preferred_element_type=jnp.float32
    )
    queries = queries.reshape(tile_rows, heads_count, head_width)
    keys_proj = key_side[:, :width].reshape(tile_cols, heads_count, head_width)
    values_proj = key_side[:, width:].reshape(tile_cols, heads_count, head_width)
    scores = jnp.einsum("ihd,jhd->ihj", queries, keys_proj) / math.sqrt(
        head_width
    ) + biases.transpose(0, 2, 1)
    scores = jnp.where(token_mask[None, None, :] > 0, scores, -1000000000.0)
    local_top = jnp.max(scores, axis=-1)
    weights = jnp.exp(scores - local_top[..., None])
    local_total = jnp.sum(weights, axis=-1)
    local_sum = jnp.einsum("ihj,jhd->ihd", weights, values_proj).reshape(tile_rows, width)
    global_top, totals, summed = combined_all(
        (local_top, local_total, local_sum), "col", combine_parts
    )
    attended = rescale(summed, 1.0 / totals)
    gated_single = (jax.nn.sigmoid(gates) * attended).astype(jnp.bfloat16)
    single_update = jnp.dot(gated_single, attention_out, preferred_element_type=jnp.float32).astype(
        jnp.bfloat16
    )
    return (distogram, single_update)


def solution(mesh):
    in_specs = (
        P(("groups", "row"), "col", None),
        P(("groups", "row"), None),
        P(("groups", "col")),
        P(),
        P(),
        P(),
        P(),
        P(),
        P(),
        P(),
        P(),
    )
    out_specs = (P(("groups", "row"), "col", None), P(("groups", "row"), None))
    return jax.shard_map(body, mesh=mesh, in_specs=in_specs, out_specs=out_specs, check_vma=False)
```

profile of v0, /device:TPU:0, one launch (start us, length us, event | category | flops | bytes accessed | tf_op | source)
XLA Modules:
  0.0 110.0 jit_solution(11541079086078294275)
XLA Ops:
  0.7 2.0 %convert_reduce_fusion = f32[64,64]{1,0:T(8,128)S(1)} fusion(bf16[64,64,128]{2,1,0:T(8,128)(2,1)} %param.13), kind=kLoop, calls=%fused_computation.21 | loop fusion | flops 1044480 | bytes 1064960 | tf_op jit(solution)/shard_map/reduce_sum | solution.py:23
  2.6 2.3 %multiply_reduce_fusion = f32[64,64]{1,0:T(8,128)S(1)} fusion(bf16[64,64,128]{2,1,0:T(8,128)(2,1)} %param.13, f32[64,64]{1,0:T(8,128)S(1)} %broadcast_multiply_fusion), kind=kLoop, calls=%fused_computation.20 | loop fusion | flops 2093056 | bytes 1081344 | tf_op jit(solution)/shard_map/reduce_sum | solution.py:25
  5.2 1.2 %fusion.8 = bf16[4096,128]{1,0:T(8,128)(2,1)S(1)} fusion(bf16[64,64,128]{2,1,0:T(8,128)(2,1)S(1)} %copy-done.1, f32[128]{0:T(128)S(1)} %copy-done.6, f32[4096]{0:T(1024)S(1)} %rsqrt.28, f32[4096]{0:T(1024)S(1)} %div.50), kind=kLoop, calls=%fused_computation.18 | loop fusion | flops 2621440 | bytes 2130432 | tf_op jit(solution)/shard_map/convert_element_type | solution.py:65
  6.4 2.3 %fusion.52 = f32[4096,1024]{1,0:T(8,128)S(1)} fusion(bf16[4096,128]{1,0:T(8,128)(2,1)S(1)} %fusion.8, bf16[128,1024]{1,0:T(8,128)(2,1)S(1)} %copy-done.3), kind=kOutput, calls=%fused_computation.80 | convolution fusion | flops 1073741824 | bytes 18087936 | tf_op jit(solution)/shard_map/dot_general | solution.py:66
  8.8 3.5 %convolution_add_fusion = f32[4096,128]{1,0:T(8,128)} fusion(bf16[512,128]{1,0:T(8,128)(2,1)S(1)} %copy-done.7, f32[4096,1024]{1,0:T(8,128)S(1)} %fusion.52, bf16[4096,128]{1,0:T(8,128)(2,1)S(1)} %bitcast.84), kind=kOutput, calls=%fused_computation.13 | convolution fusion | flops 550502400 | bytes 20054016 | tf_op jit(solution)/shard_map/dot_general | solution.py:68
  12.3 4.0 %fusion.53 = f32[4096,64]{0,1:T(8,128)S(1)} fusion(f32[4096,128]{1,0:T(8,128)} %convolution_add_fusion, f32[128,64]{0,1:T(8,128)S(1)} %copy-done.4), kind=kOutput, calls=%fused_computation.81 | convolution fusion | flops 402653184 | bytes 3178496 | tf_op jit(solution)/shard_map/dot_general | solution.py:72
  16.3 2.0 %copy.30 = f32[4096,64]{1,0:T(8,128)} copy(f32[4096,64]{0,1:T(8,128)S(1)} %fusion.53) | data formatting | bytes 2097152 | tf_op jit(solution)/shard_map/dot_general | solution.py:72
  18.3 3.5 %reshape_reshape.8 = f32[1,64,4096]{2,0,1:T(1,128)} reshape(f32[4096,64]{1,0:T(8,128)} %copy.30) | data formatting | bytes 2097152 | tf_op jit(solution)/shard_map/reshape;reshape | solution.py:75
  21.7 4.3 %all-to-all-start = ((f32[1,64,4096]{2,0,1:T(1,128)}), f32[1,64,4096]{2,0,1:T(1,128)S(1)}, u32[]{:S(2)}, u32[]{:S(2)}) async-start(f32[1,64,4096]{2,0,1:T(1,128)} %reshape_reshape.8), calls=%async_computation | async-start | bytes 2097152 | tf_op jit(solution)/shard_map/all_to_all | solution.py:76
  26.1 0.1 convert_reduce_fusion.2
  26.2 20.4 %psum.7 = bf16[64,384]{1,0:T(8,128)(2,1)S(1)} all-reduce(bf16[64,384]{1,0:T(8,128)(2,1)S(1)} %broadcast_select_fusion), channel_id=1, replica_groups=mesh['groups'=2,'row'=4,'col'=4] {'row'}, use_global_device_ids=true, to_apply=%region_6.7 | all-reduce | flops 24576 | bytes 98304 | tf_op jit(solution)/shard_map/psum | solution.py:11
  46.6 0.1 convert_reduce_fusion.1
  46.7 0.2 fusion.31
  46.9 0.2 fusion.34
  47.1 1.3 %fusion.18 = bf16[64,768]{1,0:T(8,128)(2,1)S(1)} fusion(bf16[384,1536]{1,0:T(8,128)(2,1)} %param.22, bf16[64,384]{1,0:T(8,128)(2,1)S(1)} %psum.7, f32[64]{0:T(128)S(1)} %add_rsqrt_fusion.1, f32[64]{0:T(128)S(1)} %broadcast_multiply_fusion.1, f32[384]{0:T(512)S(1)} %copy-done.8), kind=kOutput, calls=%fused_computation.35 | convolution fusion | flops 37871616 | bytes 739328 | tf_op jit(solution)/shard_map/dot_general | solution.py:92
  48.5 1.3 %fusion.22 = bf16[64,384]{0,1:T(8,128)(2,1)S(1)} fusion(bf16[384,1536]{1,0:T(8,128)(2,1)} %param.22, bf16[64,384]{1,0:T(8,128)(2,1)S(1)} %copy-done.2, f32[384]{0:T(512)S(1)} %copy-done.8, f32[64]{0:T(128)S(1)} %add_rsqrt_fusion.2, f32[64]{0:T(128)S(1)} %broadcast_multiply_fusion.2), kind=kOutput, calls=%fused_computation.40 | convolution fusion | flops 18997248 | bytes 395264 | tf_op jit(solution)/shard_map/dot_general | solution.py:90
  49.8 3.4 %fusion.54 = f32[4096,16]{0,1:T(8,128)S(1)} fusion(f32[4096,128]{1,0:T(8,128)} %convolution_add_fusion, f32[128,16]{0,1:T(8,128)S(1)} %copy-done.5), kind=kOutput, calls=%fused_computation.82 | convolution fusion | flops 100663296 | bytes 2367488 | tf_op jit(solution)/shard_map/dot_general | solution.py:69
  53.3 1.6 %copy.47 = f32[1,64,4096]{2,1,0:T(8,128)} copy(f32[1,64,4096]{2,0,1:T(1,128)S(1)} %all-to-all-done) | data formatting | bytes 2097152
  54.9 4.4 %all-to-all-start.1 = ((f32[4,16,4096]{2,1,0:T(8,128)}), f32[4,16,4096]{2,1,0:T(8,128)}, u32[]{:S(2)}, u32[]{:S(2)}) async-start(f32[4,16,4096]{2,1,0:T(8,128)} %bitcast.85), calls=%async_computation.1 | async-start | bytes 2097152 | tf_op jit(solution)/shard_map/all_to_all | solution.py:78
  59.3 0.2 reshape.111
  59.5 0.2 copy.35
  59.7 0.1 copy.33
  59.9 0.1 copy.36
  60.0 0.3 fusion.51
  60.3 0.2 fusion.20
  60.6 0.1 copy.38
  60.7 6.9 %all_gather.19 = f32[4,64,384]{2,1,0:T(8,128)S(1)} all-gather(f32[1,64,384]{2,1,0:T(8,128)S(1)} %copy.38), channel_id=1, replica_groups=mesh['groups'=2,'row'=4,'col'=4] {'col'}, dimensions={0}, use_global_device_ids=true | all-gather | bytes 491520 | tf_op jit(solution)/shard_map/all_gather | solution.py:15
  67.6 0.1 copy.39
  67.8 5.2 %all-gather.2 = f32[4,64,16]{1,2,0:T(8,128)S(1)} all-gather(f32[1,64,16]{1,2,0:T(8,128)S(1)} %bitcast.90), channel_id=2, replica_groups=mesh['groups'=2,'row'=4,'col'=4] {'col'}, dimensions={0}, use_global_device_ids=true | all-gather | bytes 20480 | tf_op jit(solution)/shard_map/all_gather | solution.py:15
  73.0 0.1 fusion.21
  73.1 5.2 %all-gather.3 = f32[4,64,16]{1,2,0:T(8,128)S(1)} all-gather(f32[1,64,16]{1,2,0:T(8,128)S(1)} %bitcast.92), channel_id=3, replica_groups=mesh['groups'=2,'row'=4,'col'=4] {'col'}, dimensions={0}, use_global_device_ids=true | all-gather | bytes 20480 | tf_op jit(solution)/shard_map/all_gather | solution.py:15
  78.3 3.8 %all-to-all-done.1 = f32[4,16,4096]{2,1,0:T(8,128)} async-done(((f32[4,16,4096]{2,1,0:T(8,128)}), f32[4,16,4096]{2,1,0:T(8,128)}, u32[]{:S(2)}, u32[]{:S(2)}) %all-to-all-start.1) | async-done | bytes 1048608 | tf_op jit(solution)/shard_map/all_to_all | solution.py:78
  82.0 4.3 %all-to-all-start.2 = ((f32[4,16,4096]{2,1,0:T(8,128)}), f32[4,16,4096]{2,1,0:T(8,128)}, u32[]{:S(2)}, u32[]{:S(2)}) async-start(f32[4,16,4096]{2,1,0:T(8,128)} %all-to-all-done.1), calls=%async_computation.2 | async-start | bytes 2097152 | tf_op jit(solution)/shard_map/all_to_all | solution.py:77
  86.3 0.8 while.14
  86.4 0.1 copy.49
  86.5 0.1 fusion.69
  86.7 0.1 copy.49
  86.9 0.1 copy.49
  87.2 2.2 %reshape_reshape.6 = f32[64,64,64]{1,0,2:T(8,128)} reshape(f32[4096,64]{0,1:T(8,128)S(1)} %fusion.53) | data formatting | bytes 2097152 | tf_op jit(solution)/shard_map/reshape;reshape | solution.py:85
  89.3 3.3 %copy.32 = f32[64,64,64]{2,0,1:T(8,128)S(1)} copy(f32[64,64,64]{1,0,2:T(8,128)} %reshape_reshape.6) | data formatting | bytes 2097152 | tf_op jit(solution)/shard_map/reshape;reshape | solution.py:85
  92.7 0.1 copy.41
  92.8 0.1 copy.42
  92.9 2.0 %convolution_convert_fusion = bf16[64,384]{1,0:T(8,128)(2,1)} fusion(bf16[384,384]{1,0:T(8,128)(2,1)S(1)} %copy-done, bf16[384,1536]{1,0:T(8,128)(2,1)} %param.22, f32[64,384]{1,0:T(8,128)S(1)} %copy.41, f32[64,384]{1,0:T(8,128)S(1)} %copy.42, bf16[64,384]{1,0:T(8,128)(2,1)S(1)} %copy-done.2, f32[384]{0:T(512)S(1)} %copy-done.8, ...), kind=kOutput, calls=%fused_computation.31 | convolution fusion | flops 38043648 | bytes 886784 | tf_op jit(solution)/shard_map/dot_general | solution.py:111
  94.9 5.9 %all-to-all-done.2 = f32[4,16,4096]{2,1,0:T(8,128)} async-done(((f32[4,16,4096]{2,1,0:T(8,128)}), f32[4,16,4096]{2,1,0:T(8,128)}, u32[]{:S(2)}, u32[]{:S(2)}) %all-to-all-start.2) | async-done | bytes 1048608 | tf_op jit(solution)/shard_map/all_to_all | solution.py:77
  100.8 3.1 %reshape.108 = f32[64,64,64]{2,1,0:T(8,128)} reshape(f32[4,16,4096]{2,1,0:T(8,128)} %all-to-all-done.2) | data formatting | bytes 2097152 | tf_op jit(solution)/shard_map/reshape | solution.py:84
  103.9 2.8 %fusion.50 = (f32[64,64]{0,1:T(8,128)S(1)}, f32[64,64,64]{2,0,1:T(8,128)S(1)}) fusion(f32[64,64,64]{2,0,1:T(8,128)S(1)} %copy.32, f32[64,64,64]{2,1,0:T(8,128)} %reshape.108), kind=kOutput, calls=%fused_computation.78 | output fusion | flops 786495 | bytes 3162112 | tf_op jit(solution)/shard_map/sub | solution.py:86
  106.7 0.7 broadcast_divide_fusion
  107.4 2.5 %copy.43 = f32[64,64,64]{2,1,0:T(8,128)} copy(f32[64,64,64]{2,0,1:T(8,128)S(1)} %broadcast_divide_fusion) | data formatting | bytes 2097152
  (48 shorter events, 0.6 us)
Async XLA Ops:
  0.6 92.3 %copy-start = (bf16[384,384]{1,0:T(8,128)(2,1)S(1)}, bf16[384,384]{1,0:T(8,128)(2,1)}, u32[]{:S(2)}) copy-start(bf16[384,384]{1,0:T(8,128)(2,1)} %param.23) | copy-start | bytes 884740
  0.6 4.5 %copy-start.1 = (bf16[64,64,128]{2,1,0:T(8,128)(2,1)S(1)}, bf16[64,64,128]{2,1,0:T(8,128)(2,1)}, u32[]{:S(2)}) copy-start(bf16[64,64,128]{2,1,0:T(8,128)(2,1)} %param.13) | copy-start | bytes 3145732
  0.7 4.5 %copy-start.6 = (f32[128]{0:T(128)S(1)}, f32[128]{0:T(128)}, u32[]{:S(2)}) copy-start(f32[128]{0:T(128)} %param.16) | copy-start | bytes 1540
  0.7 5.7 %copy-start.3 = (bf16[128,1024]{1,0:T(8,128)(2,1)S(1)}, bf16[128,1024]{1,0:T(8,128)(2,1)}, u32[]{:S(2)}) copy-start(bf16[128,1024]{1,0:T(8,128)(2,1)} %param.17) | copy-start | bytes 786436
  6.4 2.3 %copy-start.7 = (bf16[512,128]{1,0:T(8,128)(2,1)S(1)}, bf16[512,128]{1,0:T(8,128)(2,1)}, u32[]{:S(2)}) copy-start(bf16[512,128]{1,0:T(8,128)(2,1)} %param.18) | copy-start | bytes 393220
  8.8 3.5 %copy-start.4 = (f32[128,64]{0,1:T(8,128)S(1)}, f32[128,64]{0,1:T(8,128)}, u32[]{:S(2)}) copy-start(f32[128,64]{0,1:T(8,128)} %param.20) | copy-start | bytes 98308
  18.2 7.8 %copy-start.2 = (bf16[64,384]{1,0:T(8,128)(2,1)S(1)}, bf16[64,384]{1,0:T(8,128)(2,1)}, u32[]{:S(2)}) copy-start(bf16[64,384]{1,0:T(8,128)(2,1)} %param.14) | copy-start | bytes 147460
  18.3 28.9 %copy-start.8 = (f32[384]{0:T(512)S(1)}, f32[384]{0:T(512)}, u32[]{:S(2)}) copy-start(f32[384]{0:T(512)} %param.21) | copy-start | bytes 4612
  21.7 28.1 %copy-start.5 = (f32[128,16]{0,1:T(8,128)S(1)}, f32[128,16]{0,1:T(8,128)}, u32[]{:S(2)}) copy-start(f32[128,16]{0,1:T(8,128)} %param.19) | copy-start | bytes 24580
  21.7 31.6 %all-to-all-start = ((f32[1,64,4096]{2,0,1:T(1,128)}), f32[1,64,4096]{2,0,1:T(1,128)S(1)}, u32[]{:S(2)}, u32[]{:S(2)}) async-start(f32[1,64,4096]{2,0,1:T(1,128)} %reshape_reshape.8), calls=%async_computation | async-start | bytes 2097152 | tf_op jit(solution)/shard_map/all_to_all | solution.py:76
  53.3 6.0 %copy-start.9 = (s32[64]{0:T(128)S(1)}, s32[64]{0:T(128)}, u32[]{:S(2)}) copy-start(s32[64]{0:T(128)} %param.15) | copy-start | bytes 772
  54.9 27.2 %all-to-all-start.1 = ((f32[4,16,4096]{2,1,0:T(8,128)}), f32[4,16,4096]{2,1,0:T(8,128)}, u32[]{:S(2)}, u32[]{:S(2)}) async-start(f32[4,16,4096]{2,1,0:T(8,128)} %bitcast.85), calls=%async_computation.1 | async-start | bytes 2097152 | tf_op jit(solution)/shard_map/all_to_all | solution.py:78
  82.0 18.8 %all-to-all-start.2 = ((f32[4,16,4096]{2,1,0:T(8,128)}), f32[4,16,4096]{2,1,0:T(8,128)}, u32[]{:S(2)}, u32[]{:S(2)}) async-start(f32[4,16,4096]{2,1,0:T(8,128)} %all-to-all-done.1), calls=%async_computation.2 | async-start | bytes 2097152 | tf_op jit(solution)/shard_map/all_to_all | solution.py:77
where the time goes:
time: 111 us; the launch traced here: 110 us
  blocking collectives  37.8 us (34%)
  local copies, waits for them, and re-layouts  19.9 us (18%)
  matrix products  18.4 us (17%)
  starting transfers between devices  13 us (12%)
  other arithmetic  10.1 us (9%)
  waiting for transfers between devices  9.7 us (9%)
    psum x1, blocking collectives, from_root(): return lax.psum(kept, axis)  20.4 us
    all_gather x3, blocking collectives, combined_all(): pieces = jax.tree.map(lambda part: lax.all_gather(part, axis), value)  17.3 us
    all_to_all x1, waiting for transfers between devices, body(): lax.all_to_all(lax.all_to_all(spread, 'row', split_axis=0, concat_axis=0,...  5.93 us
    another operation x2, local copies, waits for them, and re-layouts, body(): symmetric = halves.reshape(tile_rows, tile_cols, bins_count) + mirrored  5.48 us
    all_to_all x1, starting transfers between devices, body(): lax.all_to_all(spread, 'row', split_axis=0, concat_axis=0, tiled=True)  4.42 us
    all_to_all x1, starting transfers between devices, body(): lax.all_to_all(stacked, 'col', split_axis=1, concat_axis=0, tiled=True)  4.34 us
    all_to_all x1, starting transfers between devices, body(): lax.all_to_all(lax.all_to_all(spread, 'row', split_axis=0, concat_axis=0,...  4.26 us
    unnamed x22, local copies, waits for them, and re-layouts  4.17 us
  transfers between devices with their start and end apart: 3, of which 2 were waited for; matrix products, arithmetic and copies ran while one was open for 15% of the time, Pallas kernels for 0%

commit v1 on v0

v1 whole, which is shorter than its diff:
```python
import functools
import math

import jax
import jax.numpy as jnp
from jax import lax
from jax.experimental import pallas as pl
from jax.experimental.pallas import tpu as pltpu
from jax.sharding import PartitionSpec as P

LANES = 128
CODE_TOP = 32767.0
VMEM_LIMIT = 56 * 1024 * 1024


def full_spec(shape):
    return pl.BlockSpec(shape, lambda *_: (0,) * len(shape))


def call(kernel, outs, args, scratch=(), aliases=None, out_specs=None, in_specs=None):
    return pl.pallas_call(
        kernel,
        grid=(1,),
        out_shape=outs,
        in_specs=in_specs or [full_spec(a.shape) for a in args],
        out_specs=out_specs or jax.tree.map(lambda o: full_spec(o.shape), outs),
        scratch_shapes=list(scratch),
        input_output_aliases=aliases or {},
        compiler_params=pltpu.CompilerParams(vmem_limit_bytes=VMEM_LIMIT),
    )(*args)


def normed(values, gain):
    average = jnp.mean(values, axis=-1, keepdims=True)
    centered = values - average
    variance = jnp.mean(centered * centered, axis=-1, keepdims=True)
    return (centered * lax.rsqrt(variance + 1e-05) * gain).astype(jnp.bfloat16)


def dot(a, b):
    return jnp.dot(a, b, preferred_element_type=jnp.float32)


def dot_t(a, b):
    return lax.dot_general(a, b, (((1,), (1,)), ((), ())), preferred_element_type=jnp.float32)


def split(value):
    high = value.astype(jnp.bfloat16)
    return high, (value - high.astype(jnp.float32)).astype(jnp.bfloat16)


def lane_index(shape):
    return lax.broadcasted_iota(jnp.int32, shape, len(shape) - 1)


def pair_kernel(
    step,
    pair_ref,
    gain_ref,
    in_ref,
    out_ref,
    bias_ref,
    bin_ref,
    heads_ref,
    code_ref,
    flat_weight,
    hidden_weight,
):
    rows, cols, _ = pair_ref.shape
    bins, heads = bin_ref.shape[1], bias_ref.shape[1]
    hidden = out_ref.shape[0]
    flat_weight[...] = jnp.zeros_like(flat_weight)
    flat_weight[:, :bins] = bin_ref[...] - bin_ref[:, bins - 1 :]
    flat_weight[:, bins : bins + heads] = bias_ref[...]
    weight = flat_weight[...]
    high = weight.astype(jnp.bfloat16)
    rest = weight - high.astype(jnp.float32)
    middle = rest.astype(jnp.bfloat16)
    low = (rest - middle.astype(jnp.float32)).astype(jnp.bfloat16)
    parts = dot(out_ref[...], jnp.concatenate([high, middle, low], axis=1))
    folded = parts[:, :LANES] + parts[:, LANES : 2 * LANES] + parts[:, 2 * LANES :]
    folded_high, folded_low = split(folded)
    hidden_weight[:hidden, :LANES] = folded_high
    hidden_weight[:hidden, LANES:] = folded_low
    hidden_weight[hidden:, :LANES] = high
    hidden_weight[hidden:, LANES:] = middle
    gain = gain_ref[...]
    for start in range(0, rows, step):
        tokens = pair_ref[start : start + step].reshape(step * cols, -1)
        inner = normed(tokens.astype(jnp.float32), gain)
        both = dot(inner, in_ref[...])
        gate = both[:, :hidden] * 0.5
        gated = (gate * (1.0 + jnp.tanh(gate)) * both[:, hidden:]).astype(jnp.bfloat16)
        twice = dot(jnp.concatenate([gated, tokens], axis=1), hidden_weight[...])
        heads_ref[start * cols : (start + step) * cols, :] = twice[:, :LANES] + twice[:, LANES:]
    half = rows // 2
    lanes = lane_index((half, LANES))
    for col in range(cols):
        first = heads_ref[pl.ds(col, half, stride=cols), :]
        second = heads_ref[pl.ds(half * cols + col, half, stride=cols), :]
        packed = jnp.where(lanes < bins, first, pltpu.roll(second, bins, 1))
        top = jnp.max(jnp.abs(packed), axis=1, keepdims=True)
        power = jnp.ceil(jnp.log2(jnp.maximum(top, 1e-30)))
        code = jnp.where(
            lanes % bins == bins - 1, power, packed * (jnp.exp2(-power) * CODE_TOP)
        )
        code_ref[col] = jnp.round(code).astype(jnp.int32).astype(jnp.int16)


def softmax_kernel(step, first_ref, second_ref, code_ref, *refs):
    out_ref = refs[-1]
    rows, cols, bins = out_ref.shape
    half = cols // 2
    lanes = lane_index((step * half, LANES))
    for start in range(0, rows, step):
        code = code_ref[start : start + step].reshape(step * half, LANES)
        code = code.astype(jnp.int32).astype(jnp.float32)
        power = jnp.sum(jnp.where(lanes == bins - 1, code, 0.0), axis=1, keepdims=True)
        other = jnp.where(lanes % bins == bins - 1, 0.0, code * (jnp.exp2(power) * (1.0 / CODE_TOP)))
        for part, own_ref in enumerate((first_ref, second_ref)):
            mirrored = other if part == 0 else pltpu.roll(other, bins, 1)
            logits = own_ref[start * half : (start + step) * half, :] + mirrored
            logits = jnp.where(lanes < bins, logits, -jnp.inf)
            top = jnp.max(logits, axis=1, keepdims=True)
            raised = jnp.exp(logits - top)
            share = raised / jnp.sum(raised, axis=1, keepdims=True)
            out_ref[start : start + step, part * half : (part + 1) * half, :] = share[
                :, :bins
            ].reshape(step, half, bins)


def attention_kernel(
    bins,
    single_ref,
    keys_ref,
    mask_ref,
    gain_ref,
    in_ref,
    first_ref,
    second_ref,
    part_ref,
    gates_ref,
    scores,
):
    rows, width = single_ref.shape
    cols = keys_ref.shape[0]
    heads = scores.shape[1]
    head_width = width // heads
    half = cols // 2
    gain = gain_ref[...]
    query_inner = normed(single_ref[...].astype(jnp.float32), gain)
    key_inner = normed(keys_ref[...].astype(jnp.float32), gain)
    queries = dot(query_inner, in_ref[:, :width]) * (1.0 / math.sqrt(head_width))
    gates_ref[...] = jax.nn.sigmoid(dot(query_inner, in_ref[:, 3 * width :]))
    keys_proj = dot(key_inner, in_ref[:, width : 2 * width]).astype(jnp.bfloat16)
    values_proj = dot(key_inner, in_ref[:, 2 * width : 3 * width]).astype(jnp.bfloat16)
    shape = (heads, width)
    lane = lane_index(shape)
    head = lax.broadcasted_iota(jnp.int32, shape, 0)
    own_head = jnp.where((lane >= head * head_width) & (lane < (head + 1) * head_width), 1.0, 0.0)
    spread = (queries[:, None, :] * own_head[None]).astype(jnp.bfloat16)
    scores[...] = dot_t(spread.reshape(rows * heads, width), keys_proj).reshape(rows, heads, cols)
    shape = (heads, 2 * LANES)
    lane = lane_index(shape) % LANES
    pick = (lane == lax.broadcasted_iota(jnp.int32, shape, 0) + bins).astype(jnp.bfloat16)
    for row in range(rows):
        block = jnp.concatenate(
            [ref[row * half : (row + 1) * half, :] for ref in (first_ref, second_ref)], axis=0
        )
        scores[row] += dot_t(pick, jnp.concatenate(split(block), axis=1))
    kept = jnp.where(mask_ref[...] > 0, scores[...].reshape(rows * heads, cols), -1000000000.0)
    top = jnp.max(kept, axis=-1, keepdims=True)
    weights = jnp.exp(kept - top)
    total = jnp.sum(weights, axis=-1, keepdims=True)
    summed = dot((weights * (1.0 / total)).astype(jnp.bfloat16), values_proj)
    summed = jnp.sum(summed.reshape(rows, heads, width) * own_head[None], axis=1)
    part_ref[:, :width] = summed.astype(jnp.bfloat16)
    level = top + jnp.log(total)
    high = level.astype(jnp.bfloat16).astype(jnp.float32)
    middle = (level - high).astype(jnp.bfloat16).astype(jnp.float32)
    low = level - high - middle
    shape = (heads, LANES)
    lane = lane_index(shape)
    head = lax.broadcasted_iota(jnp.int32, shape, 0)
    spread = jnp.zeros((rows, heads, LANES), jnp.float32)
    for place, piece in enumerate((high, middle, low)):
        at = (lane == head + place * heads).astype(jnp.float32)
        spread += piece.reshape(rows, heads, 1) * at[None]
    part_ref[:, width:] = jnp.sum(spread, axis=1).astype(jnp.bfloat16)


def joined_kernel(heads, parts_ref, gates_ref, out_weight_ref, out_ref):
    count, rows, _ = parts_ref.shape
    width = gates_ref.shape[1]
    head_width = width // heads
    shape = (LANES, width)
    lane = lane_index(shape)
    row = lax.broadcasted_iota(jnp.int32, shape, 0)
    head = row % heads
    spread = (
        (lane >= head * head_width) & (lane < (head + 1) * head_width) & (row < 3 * heads)
    ).astype(jnp.bfloat16)
    levels = [dot(parts_ref[k, :, width:], spread) for k in range(count)]
    top = functools.reduce(jnp.maximum, levels)
    total, summed = 0.0, 0.0
    for k in range(count):
        factor = jnp.exp(levels[k] - top)
        total += factor
        summed += factor * parts_ref[k, :, :width].astype(jnp.float32)
    gated = (gates_ref[...] * (summed / total)).astype(jnp.bfloat16)
    out_ref[...] = dot(gated, out_weight_ref[...]).astype(jnp.bfloat16)


def body(
    row_count,
    col_count,
    pair,
    single,
    token_mask,
    pair_gain,
    transition_in,
    transition_out,
    bias_weight,
    bin_weight,
    single_gain,
    attention_in,
    attention_out,
):
    rows, cols, channels = pair.shape
    width = single.shape[1]
    heads, bins = bias_weight.shape[1], bin_weight.shape[1]
    hidden = transition_out.shape[0]
    half = cols // 2
    mirror = [
        (r * col_count + c, c * col_count + r) for r in range(row_count) for c in range(col_count)
    ]

    def mirrored(value):
        return lax.ppermute(value, ("row", "col"), mirror)

    keys = mirrored(single)
    shared = (
        pair_gain.reshape(1, -1),
        transition_in,
        transition_out,
        bias_weight,
        bin_weight,
    )
    own, received = [], []
    for part in range(2):
        spec = pl.BlockSpec((rows, half, channels), lambda _, part=part: (0, part, 0))
        logits, code = call(
            functools.partial(pair_kernel, 8),
            (
                jax.ShapeDtypeStruct((rows * half, LANES), jnp.float32),
                jax.ShapeDtypeStruct((half, rows // 2, LANES), jnp.int16),
            ),
            (pair, *shared),
            scratch=(
                pltpu.VMEM((channels, LANES), jnp.float32),
                pltpu.VMEM((hidden + channels, 2 * LANES), jnp.bfloat16),
            ),
            in_specs=[spec] + [full_spec(a.shape) for a in shared],
        )
        own.append(logits)
        received.append(mirrored(code))

    part_sums, gates = call(
        functools.partial(attention_kernel, bins),
        (
            jax.ShapeDtypeStruct((rows, width + LANES), jnp.bfloat16),
            jax.ShapeDtypeStruct((rows, width), jnp.float32),
        ),
        (
            single,
            keys,
            token_mask.reshape(1, -1),
            single_gain.reshape(1, -1),
            attention_in,
            *own,
        ),
        scratch=(pltpu.VMEM((rows, heads, cols), jnp.float32),),
    )
    gathered = lax.all_gather(part_sums, "col")
    single_update = call(
        functools.partial(joined_kernel, heads),
        jax.ShapeDtypeStruct((rows, width), jnp.bfloat16),
        (gathered, gates, attention_out),
    )
    distogram = None
    out = jax.ShapeDtypeStruct((rows, cols, bins), jnp.float32)
    count = rows // 2
    for part in range(2):
        own_spec = pl.BlockSpec((count * half, LANES), lambda _, part=part: (part, 0))
        args, specs = [*own, received[part]], [own_spec, own_spec, full_spec(received[part].shape)]
        if part:
            args.append(distogram)
            specs.append(pl.BlockSpec(memory_space=pl.ANY))
        distogram = call(
            functools.partial(softmax_kernel, 4),
            out,
            args,
            in_specs=specs,
            out_specs=pl.BlockSpec((count, cols, bins), lambda _, part=part: (part, 0, 0)),
            aliases={3: 0} if part else {},
        )
    return (distogram, single_update)


def solution(mesh):
    in_specs = (
        P(("groups", "row"), "col", None),
        P(("groups", "row"), None),
        P(("groups", "col")),
        P(),
        P(),
        P(),
        P(),
        P(),
        P(),
        P(),
        P(),
    )
    out_specs = (P(("groups", "row"), "col", None), P(("groups", "row"), None))
    own = functools.partial(body, mesh.shape["row"], mesh.shape["col"])
    return jax.shard_map(own, mesh=mesh, in_specs=in_specs, out_specs=out_specs, check_vma=False)
```

time: 111 us -> 67.7 us (0.61)
  Pallas kernels: 0 us -> 26.6 us
  matrix products: 18.4 us -> 0 us
  local copies, waits for them, and re-layouts: 19.9 us -> 5.49 us
  other arithmetic: 10.1 us -> 0 us
  waiting for transfers between devices: 9.7 us -> 0.01 us
  starting transfers between devices: 13 us -> 3.85 us
  blocking collectives: 37.8 us -> 30.6 us
    pallas_call x0 -> x6, Pallas kernels: none -> 26.6 us  [call(): pl.pallas_call(kernel, grid=(1,), out_shape=outs, in_specs=in_specs or [f...]
    psum x1 -> x0, blocking collectives: 20.4 us -> none  [from_root(): return lax.psum(kept, axis)]
    dot_general x9 -> x0, matrix products: 18.4 us -> none  [the longest x1 3.97 us: body(): jnp.dot(updated, bin_weight, precision=lax.Precision.HIGHEST)]
    all_gather x3 -> x1, blocking collectives: 17.3 us -> 30.6 us  [body(): gathered = lax.all_gather(part_sums, 'col')]
    all_to_all x3 -> x0, starting transfers between devices: 13 us -> none  [the longest x1 4.42 us: body(): lax.all_to_all(spread, 'row', split_axis=0, concat_axis=0, tiled=True)]
    all_to_all x3 -> x0, waiting for transfers between devices: 9.7 us -> none  [the longest x1 5.93 us: body(): lax.all_to_all(lax.all_to_all(spread, 'row', split_axis=0, concat_axis=0,...]
    another operation x4 -> x0, local copies, waits for them, and re-layouts: 9.05 us -> none  [the longest x2 5.48 us: body(): symmetric = halves.reshape(tile_rows, tile_cols, bins_count) + mirrored]
    reduce_sum x7 -> x0, other arithmetic: 4.98 us -> none  [the longest x3 2.7 us: layer_norm(): variance = jnp.mean(centered * centered, axis=-1, keepdims=True)]
  transfers between devices with their start and end apart: 3 -> 3, of which waited for: 2 -> 0; matrix products, arithmetic and copies ran while one was open for 15% -> 1% of each run, Pallas kernels for 0% -> 25%
where the time goes in v1:
time: 67.7 us; the launch traced here: 67.2 us
  blocking collectives  30.6 us (45%)
  Pallas kernels  26.6 us (39%)
  local copies, waits for them, and re-layouts  5.49 us (8%)
  starting transfers between devices  3.85 us (6%)
    all_gather x1, blocking collectives, body(): gathered = lax.all_gather(part_sums, 'col')  30.6 us
    pallas_call x6, Pallas kernels, call(): pl.pallas_call(kernel, grid=(1,), out_shape=outs, in_specs=in_specs or [f...  26.6 us
    unnamed x12, local copies, waits for them, and re-layouts  4.96 us
    ppermute x3, starting transfers between devices, mirrored(): return lax.ppermute(value, ('row', 'col'), mirror)  3.85 us
  transfers between devices with their start and end apart: 3, of which 0 were waited for; matrix products, arithmetic and copies ran while one was open for 1% of the time, Pallas kernels for 25%

profile of v1, /device:TPU:0, one launch (start us, length us, event | category | flops | bytes accessed | tf_op | source)
XLA Modules:
  0.0 67.2 jit_solution(5775085432126715281)
XLA Ops:
  0.6 0.0 copy-start.2
  0.6 0.0 copy-start.4
  0.7 1.4 %copy.14.bias_ref = f32[128,16]{1,0:T(8,128)} copy(f32[128,16]{0,1:T(8,128)} %param.17) | data formatting | bytes 16384 | tf_op args[6]
  2.1 1.5 %copy.15.bin_ref = f32[128,64]{1,0:T(8,128)} copy(f32[128,64]{0,1:T(8,128)} %param.18) | data formatting | bytes 65536 | tf_op args[7]
  3.6 5.3 %shard_map.122 = (f32[2048,128]{1,0:T(8,128)}, s16[32,32,128]{2,1,0:T(8,128)(2,1)}) custom-call(bf16[64,64,128]{2,1,0:T(8,128)(2,1)} %pair_ref.3, f32[1,128]{1,0:T(1,128)} %bitcast.4, bf16[128,1024]{1,0:T(8,128)(2,1)} %in_ref.4, bf16[512,128]{1,0:T(8,128)(2,1)} %out_ref.3, f32[128,16]{1,0:T(8,128)} %copy.14.bias_ref, f32[128,64]{1,0:T(8,128)} %copy.15.bin_ref), custom_call_target="tpu_custom_call" | custom-call | tf_op jit(solution)/shard_map/pallas_call | solution.py:21
  8.9 1.6 %collective-permute-start.1 = (s16[32,32,128]{2,1,0:T(8,128)(2,1)}, s16[32,32,128]{2,1,0:T(8,128)(2,1)S(1)}, u32[]{:S(2)}, u32[]{:S(2)}) collective-permute-start(s16[32,32,128]{2,1,0:T(8,128)(2,1)} %get-tuple-element.11), channel_id=1, source_target_pairs={{0,0},{1,4},{2,8},{3,12},{4,1},{5,5},{6,9},{7,13},{8,2},{9,6},{10,... | collective-permute-start | bytes 786440 | tf_op jit(solution)/shard_map/ppermute | solution.py:240
  10.5 5.4 %shard_map.123 = (f32[2048,128]{1,0:T(8,128)}, s16[32,32,128]{2,1,0:T(8,128)(2,1)}) custom-call(bf16[64,64,128]{2,1,0:T(8,128)(2,1)} %pair_ref.3, f32[1,128]{1,0:T(1,128)} %bitcast.5, bf16[128,1024]{1,0:T(8,128)(2,1)} %in_ref.4, bf16[512,128]{1,0:T(8,128)(2,1)} %out_ref.3, f32[128,16]{1,0:T(8,128)} %copy.14.bias_ref, f32[128,64]{1,0:T(8,128)} %copy.15.bin_ref), custom_call_target="tpu_custom_call" | custom-call | tf_op jit(solution)/shard_map/pallas_call | solution.py:21
  15.9 1.6 %collective-permute-start = (s16[32,32,128]{2,1,0:T(8,128)(2,1)}, s16[32,32,128]{2,1,0:T(8,128)(2,1)S(1)}, u32[]{:S(2)}, u32[]{:S(2)}) collective-permute-start(s16[32,32,128]{2,1,0:T(8,128)(2,1)} %get-tuple-element.10), channel_id=1, source_target_pairs={{0,0},{1,4},{2,8},{3,12},{4,1},{5,5},{6,9},{7,13},{8,2},{9,6},{10,... | collective-permute-start | bytes 786440 | tf_op jit(solution)/shard_map/ppermute | solution.py:240
  17.5 0.0 copy-done.2
  17.5 0.7 collective-permute-start.2
  18.1 0.0 copy-done.4
  18.1 0.5 reshape.15.gain_ref
  18.7 0.0 collective-permute-done.2.keys_ref
  18.7 0.0 copy-start.3
  18.7 0.6 copy-done.3
  19.3 4.5 %shard_map.126 = (bf16[64,512]{1,0:T(8,128)(2,1)}, f32[64,384]{1,0:T(8,128)}) custom-call(bf16[64,384]{1,0:T(8,128)(2,1)} %single_ref.1, bf16[64,384]{1,0:T(8,128)(2,1)} %copy-done.3, s32[1,64]{1,0:T(1,128)} %bitcast.6, f32[1,384]{1,0:T(1,128)} %reshape.15.gain_ref, bf16[384,1536]{1,0:T(8,128)(2,1)} %in_ref.5, f32[2048,128]{1,0:T(8,128)} %get-tuple-element.8.first_ref, ...), custom_call_target="tpu_custom_call" | custom-call | tf_op jit(solution)/shard_map/pallas_call | solution.py:21
  23.8 30.6 %all-gather = bf16[256,512]{1,0:T(8,128)(2,1)} all-gather(bf16[64,512]{1,0:T(8,128)(2,1)} %get-tuple-element.12), channel_id=2, replica_groups=mesh['groups'=2,'row'=4,'col'=4] {'col'}, dimensions={0}, use_global_device_ids=true | all-gather | bytes 327680 | tf_op jit(solution)/shard_map/all_gather | solution.py:285
  54.4 2.1 %shard_map.127 = bf16[64,384]{1,0:T(8,128)(2,1)} custom-call(bf16[4,64,512]{2,1,0:T(8,128)(2,1)} %bitcast.3, f32[64,384]{1,0:T(8,128)} %get-tuple-element.13.gates_ref, bf16[384,384]{1,0:T(8,128)(2,1)} %out_weight_ref.1), custom_call_target="tpu_custom_call" | custom-call | tf_op jit(solution)/shard_map/pallas_call | solution.py:21
  56.5 0.0 collective-permute-done.1.code_ref
  56.5 0.0 copy-start
  56.5 0.7 %copy-done = s16[32,32,128]{2,1,0:T(8,128)(2,1)} copy-done((s16[32,32,128]{2,1,0:T(8,128)(2,1)}, s16[32,32,128]{2,1,0:T(8,128)(2,1)S(1)}, u32[]{:S(2)}) %copy-start) | copy-done | bytes 262168
  57.2 4.6 %shard_map.124.refs_0_ = f32[64,64,64]{2,1,0:T(8,128)} custom-call(f32[2048,128]{1,0:T(8,128)} %get-tuple-element.8.first_ref, f32[2048,128]{1,0:T(8,128)} %get-tuple-element.9.second_ref, s16[32,32,128]{2,1,0:T(8,128)(2,1)} %copy-done), custom_call_target="tpu_custom_call" | custom-call | tf_op jit(solution)/shard_map/pallas_call | solution.py:21
  61.9 0.0 collective-permute-done.code_ref
  61.9 0.0 copy-start.1
  61.9 0.7 %copy-done.1 = s16[32,32,128]{2,1,0:T(8,128)(2,1)} copy-done((s16[32,32,128]{2,1,0:T(8,128)(2,1)}, s16[32,32,128]{2,1,0:T(8,128)(2,1)S(1)}, u32[]{:S(2)}) %copy-start.1) | copy-done | bytes 262168
  62.6 4.6 %shard_map.125 = f32[64,64,64]{2,1,0:T(8,128)} custom-call(f32[2048,128]{1,0:T(8,128)} %get-tuple-element.8.first_ref, f32[2048,128]{1,0:T(8,128)} %get-tuple-element.9.second_ref, s16[32,32,128]{2,1,0:T(8,128)(2,1)} %copy-done.1, f32[64,64,64]{2,1,0:T(8,128)} %shard_map.124.refs_0_), custom_call_target="tpu_custom_call", output_to_operand_aliasing={{}: (3, {})} | custom-call | tf_op jit(solution)/shard_map/pallas_call | solution.py:21
Async XLA Ops:
  0.6 16.8 %copy-start.2 = (bf16[64,384]{1,0:T(8,128)(2,1)S(1)}, bf16[64,384]{1,0:T(8,128)(2,1)}, u32[]{:S(2)}) copy-start(bf16[64,384]{1,0:T(8,128)(2,1)} %single_ref.1) | copy-start | bytes 147460
  0.6 17.5 %copy-start.4 = (f32[384]{0:T(512)S(1)}, f32[384]{0:T(512)}, u32[]{:S(2)}) copy-start(f32[384]{0:T(512)} %param.19) | copy-start | bytes 4612
  8.9 47.6 %collective-permute-start.1 = (s16[32,32,128]{2,1,0:T(8,128)(2,1)}, s16[32,32,128]{2,1,0:T(8,128)(2,1)S(1)}, u32[]{:S(2)}, u32[]{:S(2)}) collective-permute-start(s16[32,32,128]{2,1,0:T(8,128)(2,1)} %get-tuple-element.11), channel_id=1, source_target_pairs={{0,0},{1,4},{2,8},{3,12},{4,1},{5,5},{6,9},{7,13},{8,2},{9,6},{10,... | collective-permute-start | bytes 786440 | tf_op jit(solution)/shard_map/ppermute | solution.py:240
  15.9 46.0 %collective-permute-start = (s16[32,32,128]{2,1,0:T(8,128)(2,1)}, s16[32,32,128]{2,1,0:T(8,128)(2,1)S(1)}, u32[]{:S(2)}, u32[]{:S(2)}) collective-permute-start(s16[32,32,128]{2,1,0:T(8,128)(2,1)} %get-tuple-element.10), channel_id=1, source_target_pairs={{0,0},{1,4},{2,8},{3,12},{4,1},{5,5},{6,9},{7,13},{8,2},{9,6},{10,... | collective-permute-start | bytes 786440 | tf_op jit(solution)/shard_map/ppermute | solution.py:240
  17.5 1.2 %collective-permute-start.2 = (bf16[64,384]{1,0:T(8,128)(2,1)S(1)}, bf16[64,384]{1,0:T(8,128)(2,1)S(1)}, u32[]{:S(2)}, u32[]{:S(2)}) collective-permute-start(bf16[64,384]{1,0:T(8,128)(2,1)S(1)} %copy-done.2), channel_id=1, source_target_pairs={{0,0},{1,4},{2,8},{3,12},{4,1},{5,5},{6,9},{7,13},{8,2},{9,6},{10,... | collective-permute-start | bytes 147464 | tf_op jit(solution)/shard_map/ppermute | solution.py:240
  18.7 0.6 copy-start.3
  56.5 0.7 %copy-start = (s16[32,32,128]{2,1,0:T(8,128)(2,1)}, s16[32,32,128]{2,1,0:T(8,128)(2,1)S(1)}, u32[]{:S(2)}) copy-start(s16[32,32,128]{2,1,0:T(8,128)(2,1)S(1)} %collective-permute-done.1.code_ref) | copy-start | bytes 786436
  61.9 0.7 %copy-start.1 = (s16[32,32,128]{2,1,0:T(8,128)(2,1)}, s16[32,32,128]{2,1,0:T(8,128)(2,1)S(1)}, u32[]{:S(2)}) copy-start(s16[32,32,128]{2,1,0:T(8,128)(2,1)S(1)} %collective-permute-done.code_ref) | copy-start | bytes 786436

commit v2 on v1

v2 whole, which is shorter than its diff:
```python
import functools
import math

import jax
import jax.numpy as jnp
from jax import lax
from jax.experimental import pallas as pl
from jax.experimental.pallas import tpu as pltpu
from jax.sharding import PartitionSpec as P

LANES = 128
CODE_TOP = 32767.0
PAIR_STEP = 8
CODE_GROUP = 8
SOFT_STEP = 8
VMEM_LIMIT = 56 * 1024 * 1024


def near(shape, dtype):
    return pltpu.VMEM(shape, dtype)


def call(kernel, outs, args, scratch=(), far=(), aliases=None):
    def out_spec(out):
        inside = isinstance(out, type(near((8, LANES), jnp.float32)))
        return pl.BlockSpec(memory_space=pltpu.VMEM if inside else pl.ANY)

    return pl.pallas_call(
        kernel,
        out_shape=outs,
        in_specs=[
            pl.BlockSpec(memory_space=pl.ANY if k in far else pltpu.VMEM) for k in range(len(args))
        ],
        out_specs=jax.tree.map(out_spec, outs),
        scratch_shapes=list(scratch),
        input_output_aliases=aliases or {},
        compiler_params=pltpu.CompilerParams(vmem_limit_bytes=VMEM_LIMIT),
    )(
        *[
            a if k in far else pltpu.with_memory_space_constraint(a, pltpu.VMEM)
            for k, a in enumerate(args)
        ]
    )


def centered(values):
    rest = values - jnp.mean(values, axis=-1, keepdims=True)
    variance = jnp.mean(rest * rest, axis=-1, keepdims=True)
    return rest * lax.rsqrt(variance + 1e-05)


def dot(a, b):
    return jnp.dot(a, b, preferred_element_type=jnp.float32)


def dot_t(a, b):
    return lax.dot_general(a, b, (((1,), (1,)), ((), ())), preferred_element_type=jnp.float32)


def split(value):
    high = value.astype(jnp.bfloat16)
    return high, (value - high.astype(jnp.float32)).astype(jnp.bfloat16)


def lane_index(shape):
    return lax.broadcasted_iota(jnp.int32, shape, len(shape) - 1)


def fill_weights(out_ref, bias_ref, bin_ref, flat_weight, weight_ref):
    bins, heads = bin_ref.shape[0], bias_ref.shape[0]
    hidden = out_ref.shape[0]
    flat_weight[...] = jnp.zeros_like(flat_weight)
    flat_weight[:bins, :] = bin_ref[...] - bin_ref[bins - 1 :, :]
    flat_weight[bins : bins + heads, :] = bias_ref[...]
    weight = flat_weight[...].T
    high = weight.astype(jnp.bfloat16)
    rest = weight - high.astype(jnp.float32)
    middle = rest.astype(jnp.bfloat16)
    low = (rest - middle.astype(jnp.float32)).astype(jnp.bfloat16)
    parts = dot(out_ref[...], jnp.concatenate([high, middle, low], axis=1))
    folded = parts[:, :LANES] + parts[:, LANES : 2 * LANES] + parts[:, 2 * LANES :]
    folded_high, folded_low = split(folded)
    weight_ref[:hidden, :LANES] = folded_high
    weight_ref[:hidden, LANES:] = folded_low
    weight_ref[hidden:, :LANES] = high
    weight_ref[hidden:, LANES:] = middle


def pair_heads(pair_ref, gain, in_ref, weight_ref, heads_ref):
    rows, cols, channels = pair_ref.shape
    hidden = in_ref.shape[1] // 2
    for start in range(0, rows, PAIR_STEP):
        tokens = pair_ref[start : start + PAIR_STEP].reshape(PAIR_STEP * cols, channels)
        inner = centered(tokens.astype(jnp.float32)) * gain
        both = dot(inner.astype(jnp.bfloat16), in_ref[...])
        gate = both[:, :hidden] * 0.5
        gated = (gate * (1.0 + jnp.tanh(gate)) * both[:, hidden:]).astype(jnp.bfloat16)
        twice = dot(gated, weight_ref[:hidden, :]) + dot(tokens, weight_ref[hidden:, :])
        at = slice(start * cols, (start + PAIR_STEP) * cols)
        heads_ref[at, :] = twice[:, :LANES] + twice[:, LANES:]


def fill_code(bins, rows, cols, heads_ref, code_ref):
    half = rows // 2
    lanes = lane_index((half * CODE_GROUP, LANES))
    for start in range(0, cols, CODE_GROUP):
        first, second = (
            jnp.concatenate(
                [
                    heads_ref[pl.ds(top * cols + col, half, stride=cols), :]
                    for col in range(start, start + CODE_GROUP)
                ],
                axis=0,
            )
            for top in (0, half)
        )
        packed = jnp.where(lanes < bins, first, pltpu.roll(second, bins, 1))
        top = jnp.max(jnp.abs(packed), axis=1, keepdims=True)
        power = jnp.ceil(jnp.log2(jnp.maximum(top, 1e-30)))
        code = jnp.where(
            lanes % bins == bins - 1, power, packed * (jnp.exp2(-power) * CODE_TOP)
        )
        code = jnp.round(code).astype(jnp.int32).astype(jnp.int16)
        code_ref[start : start + CODE_GROUP] = code.reshape(CODE_GROUP, half, LANES)


def first_kernel(
    pair_ref,
    gain_ref,
    in_ref,
    out_ref,
    bias_ref,
    bin_ref,
    heads_ref,
    code_ref,
    later_ref,
    gain_near,
    in_near,
    weight_ref,
    tile,
    out_near,
    bias_near,
    bin_near,
    flat_weight,
    sems,
):
    rows, cols, _ = tile.shape

    def bring(source, target, sem):
        copy = pltpu.make_async_copy(source, target, sem)
        copy.start()
        return copy

    small = [
        bring(source, target, sems.at[k])
        for k, (source, target) in enumerate(
            ((bias_ref, bias_near), (bin_ref, bin_near), (out_ref, out_near))
        )
    ]
    gain_copy = bring(gain_ref, gain_near, sems.at[3])
    tile_copy = bring(pair_ref.at[:, pl.ds(0, cols)], tile, sems.at[4])
    in_copy = bring(in_ref, in_near, sems.at[5])
    later = bring(pair_ref.at[:, pl.ds(cols, cols)], later_ref, sems.at[6])
    for copy in small:
        copy.wait()
    fill_weights(out_near, bias_near, bin_near, flat_weight, weight_ref)
    gain_copy.wait()
    in_copy.wait()
    tile_copy.wait()
    gain = gain_near[...].reshape(1, -1)
    pair_heads(tile, gain, in_near, weight_ref, heads_ref)
    fill_code(bin_ref.shape[0], rows, cols, heads_ref, code_ref)
    later.wait()


def second_kernel(bins, pair_ref, gain_ref, in_ref, weight_ref, heads_ref, code_ref):
    rows, cols, _ = pair_ref.shape
    gain = gain_ref[...].reshape(1, -1)
    pair_heads(pair_ref, gain, in_ref, weight_ref, heads_ref)
    fill_code(bins, rows, cols, heads_ref, code_ref)


def softmax_kernel(part, step, first_ref, second_ref, code_ref, *refs):
    out_ref, held, sems = refs[-3:]
    rows, cols, bins = held.shape
    half = cols // 2
    lanes = lane_index((step * half, LANES))
    low = lanes < bins
    copies = []
    for start in range(0, rows, step):
        code = code_ref[start : start + step].reshape(step * half, LANES)
        code = code.astype(jnp.int32).astype(jnp.float32)
        power = jnp.sum(jnp.where(lanes == bins - 1, code, 0.0), axis=1, keepdims=True)
        other = code * (jnp.exp2(power) * (1.0 / CODE_TOP))
        other = jnp.where(lanes % bins == bins - 1, 0.0, other)
        at = pl.ds((part * rows + start) * half, step * half)
        for side, own_ref in enumerate((first_ref, second_ref)):
            mirrored = other if side == 0 else pltpu.roll(other, bins, 1)
            logits = jnp.where(low, own_ref[at, :] + mirrored, -jnp.inf)
            top = jnp.max(logits, axis=1, keepdims=True)
            raised = jnp.exp(logits - top)
            share = raised * (1.0 / jnp.sum(raised, axis=1, keepdims=True))
            held[start : start + step, side * half : (side + 1) * half, :] = share[
                :, :bins
            ].reshape(step, half, bins)
        copies.append(
            pltpu.make_async_copy(
                held.at[pl.ds(start, step)],
                out_ref.at[pl.ds(part * rows + start, step)],
                sems.at[start // step],
            )
        )
        copies[-1].start()
    for copy in copies:
        copy.wait()


def attention_kernel(
    bins,
    single_ref,
    keys_ref,
    mask_ref,
    gain_ref,
    in_ref,
    first_ref,
    second_ref,
    part_ref,
    gates_ref,
    scores,
):
    rows, width = single_ref.shape
    heads, cols = scores.shape[1:]
    head_width = width // heads
    half = cols // 2
    gain = gain_ref[...].reshape(1, -1)
    query_inner = (centered(single_ref[...].astype(jnp.float32)) * gain).astype(jnp.bfloat16)
    key_inner = (centered(keys_ref[...].astype(jnp.float32)) * gain).astype(jnp.bfloat16)
    queries = dot(query_inner, in_ref[:, :width]) * (1.0 / math.sqrt(head_width))
    gates_ref[...] = jax.nn.sigmoid(dot(query_inner, in_ref[:, 3 * width :]))
    keys_proj = dot(key_inner, in_ref[:, width : 2 * width]).astype(jnp.bfloat16)
    values_proj = dot(key_inner, in_ref[:, 2 * width : 3 * width]).astype(jnp.bfloat16)
    shape = (heads, width)
    lane = lane_index(shape)
    head = lax.broadcasted_iota(jnp.int32, shape, 0)
    own_head = jnp.where((lane >= head * head_width) & (lane < (head + 1) * head_width), 1.0, 0.0)
    spread = (queries[:, None, :] * own_head[None]).astype(jnp.bfloat16)
    scores[...] = dot_t(spread.reshape(rows * heads, width), keys_proj).reshape(rows, heads, cols)
    shape = (heads, 2 * LANES)
    lane = lane_index(shape) % LANES
    pick = (lane == lax.broadcasted_iota(jnp.int32, shape, 0) + bins).astype(jnp.bfloat16)
    for row in range(rows):
        block = jnp.concatenate(
            [ref[row * half : (row + 1) * half, :] for ref in (first_ref, second_ref)], axis=0
        )
        scores[row] += dot_t(pick, jnp.concatenate(split(block), axis=1))
    kept = jnp.where(mask_ref[...].reshape(1, -1) > 0, scores[...].reshape(rows * heads, cols), -1000000000.0)
    top = jnp.max(kept, axis=-1, keepdims=True)
    weights = jnp.exp(kept - top)
    total = jnp.sum(weights, axis=-1, keepdims=True)
    summed = dot((weights * (1.0 / total)).astype(jnp.bfloat16), values_proj)
    summed = jnp.sum(summed.reshape(rows, heads, width) * own_head[None], axis=1)
    part_ref[:, :width] = summed.astype(jnp.bfloat16)
    level = top + jnp.log(total)
    high = level.astype(jnp.bfloat16).astype(jnp.float32)
    middle = (level - high).astype(jnp.bfloat16).astype(jnp.float32)
    low = level - high - middle
    shape = (heads, LANES)
    lane = lane_index(shape)
    head = lax.broadcasted_iota(jnp.int32, shape, 0)
    spread = jnp.zeros((rows, heads, LANES), jnp.float32)
    for place, piece in enumerate((high, middle, low)):
        at = (lane == head + place * heads).astype(jnp.float32)
        spread += piece.reshape(rows, heads, 1) * at[None]
    part_ref[:, width:] = jnp.sum(spread, axis=1).astype(jnp.bfloat16)


def joined_kernel(heads, count, *refs):
    parts, (gates_ref, out_weight_ref, out_ref, held, sem) = refs[:count], refs[count:]
    width = gates_ref.shape[1]
    head_width = width // heads
    shape = (LANES, width)
    lane = lane_index(shape)
    row = lax.broadcasted_iota(jnp.int32, shape, 0)
    head = row % heads
    spread = (
        (lane >= head * head_width) & (lane < (head + 1) * head_width) & (row < 3 * heads)
    ).astype(jnp.bfloat16)
    levels = [dot(part[:, width:], spread) for part in parts]
    top = functools.reduce(jnp.maximum, levels)
    total, summed = 0.0, 0.0
    for level, part in zip(levels, parts):
        factor = jnp.exp(level - top)
        total += factor
        summed += factor * part[:, :width].astype(jnp.float32)
    gated = (gates_ref[...] * (summed / total)).astype(jnp.bfloat16)
    held[...] = dot(gated, out_weight_ref[...]).astype(jnp.bfloat16)
    copy = pltpu.make_async_copy(held, out_ref, sem)
    copy.start()
    copy.wait()


def body(
    row_count,
    col_count,
    pair,
    single,
    token_mask,
    pair_gain,
    transition_in,
    transition_out,
    bias_weight,
    bin_weight,
    single_gain,
    attention_in,
    attention_out,
):
    rows, cols, channels = pair.shape
    width = single.shape[1]
    heads, bins = bias_weight.shape[1], bin_weight.shape[1]
    hidden = transition_out.shape[0]
    half = cols // 2
    mirror = [
        (r * col_count + c, c * col_count + r) for r in range(row_count) for c in range(col_count)
    ]

    def mirrored(value):
        return lax.ppermute(value, ("row", "col"), mirror)

    bf16, f32, i16 = jnp.bfloat16, jnp.float32, jnp.int16
    heads_out = near((rows * half, LANES), f32)
    first, code, later, *kept = call(
        first_kernel,
        (
            heads_out,
            near((half, rows // 2, LANES), i16),
            near((rows, half, channels), bf16),
            near(pair_gain.shape, f32),
            near(transition_in.shape, bf16),
            near((hidden + channels, 2 * LANES), bf16),
        ),
        (pair, pair_gain, transition_in, transition_out, bias_weight.T, bin_weight.T),
        scratch=(
            pltpu.VMEM((rows, half, channels), bf16),
            pltpu.VMEM(transition_out.shape, bf16),
            pltpu.VMEM((heads, channels), f32),
            pltpu.VMEM((bins, channels), f32),
            pltpu.VMEM((LANES, channels), f32),
            pltpu.SemaphoreType.DMA((7,)),
        ),
        far=range(6),
    )
    received = [mirrored(code)]
    behind, _ = lax.optimization_barrier((single, code))
    keys = mirrored(behind)
    second, code = call(
        functools.partial(second_kernel, bins),
        (heads_out, near((half, rows // 2, LANES), i16)),
        (later, *kept),
    )
    own = (first, second)
    code, keys = lax.optimization_barrier((code, keys))
    received.append(mirrored(code))
    part_sums, gates = call(
        functools.partial(attention_kernel, bins),
        (
            near((rows, width + LANES), jnp.bfloat16),
            near((rows, width), jnp.float32),
        ),
        (single, keys, token_mask, single_gain, attention_in, *own),
        scratch=(pltpu.VMEM((rows, heads, cols), jnp.float32),),
    )
    parts = [part_sums]
    for away in range(1, col_count):
        ring = [(c, (c + away) % col_count) for c in range(col_count)]
        parts.append(lax.ppermute(part_sums, "col", ring))
    single_update = call(
        functools.partial(joined_kernel, heads, col_count),
        jax.ShapeDtypeStruct((rows, width), bf16),
        (*parts, gates, attention_out),
        scratch=(pltpu.VMEM((rows, width), bf16), pltpu.SemaphoreType.DMA),
    )
    distogram = None
    count = rows // 2
    for part in range(2):
        distogram = call(
            functools.partial(softmax_kernel, part, SOFT_STEP),
            jax.ShapeDtypeStruct((rows, cols, bins), jnp.float32),
            (*own, received[part]) + ((distogram,) if part else ()),
            scratch=(
                pltpu.VMEM((count, cols, bins), jnp.float32),
                pltpu.SemaphoreType.DMA((count // SOFT_STEP,)),
            ),
            far=(3,) if part else (),
            aliases={3: 0} if part else {},
        )
    return (distogram, single_update)


def solution(mesh):
    in_specs = (
        P(("groups", "row"), "col", None),
        P(("groups", "row"), None),
        P(("groups", "col")),
        P(),
        P(),
        P(),
        P(),
        P(),
        P(),
        P(),
        P(),
    )
    out_specs = (P(("groups", "row"), "col", None), P(("groups", "row"), None))
    own = functools.partial(body, mesh.shape["row"], mesh.shape["col"])
    return jax.shard_map(own, mesh=mesh, in_specs=in_specs, out_specs=out_specs, check_vma=False)
```

time: 67.7 us -> 40.1 us (0.59)
  blocking collectives: 30.6 us -> 0 us
  starting transfers between devices: 3.85 us -> 16.6 us
  Pallas kernels: 26.6 us -> 15.5 us
  waiting for transfers between devices: 0.01 us -> 6.85 us
  local copies, waits for them, and re-layouts: 5.49 us -> 0.03 us
    all_gather x1 -> x0, blocking collectives: 30.6 us -> none  [body(): gathered = lax.all_gather(part_sums, 'col')]
    ppermute x0 -> x3, starting transfers between devices: none -> 13.8 us  [body(): parts.append(lax.ppermute(part_sums, 'col', ring))]
    pallas_call x6, Pallas kernels: 26.6 us -> 15.5 us  [call(): pl.pallas_call(kernel, out_shape=outs, in_specs=[pl.BlockSpec(memory_spac...]
    ppermute x0 -> x3, waiting for transfers between devices: none -> 6.84 us  [body(): parts.append(lax.ppermute(part_sums, 'col', ring))]
    unnamed x12 -> x10, local copies, waits for them, and re-layouts: 4.96 us -> 0.03 us
    ppermute x3, starting transfers between devices: 3.85 us -> 2.8 us  [mirrored(): return lax.ppermute(value, ('row', 'col'), mirror)]
  transfers between devices with their start and end apart: 3 -> 6, of which waited for: 0 -> 2; matrix products, arithmetic and copies ran while one was open for 1% -> 0% of each run, Pallas kernels for 25% -> 21%
where the time goes in v2:
time: 40.1 us; the launch traced here: 39.8 us
  starting transfers between devices  16.6 us (41%)
  Pallas kernels  15.5 us (39%)
  waiting for transfers between devices  6.85 us (17%)
  between operations  0.79 us (2%)
    pallas_call x6, Pallas kernels, call(): pl.pallas_call(kernel, out_shape=outs, in_specs=[pl.BlockSpec(memory_spac...  15.5 us
    ppermute x3, starting transfers between devices, body(): parts.append(lax.ppermute(part_sums, 'col', ring))  13.8 us
    ppermute x3, waiting for transfers between devices, body(): parts.append(lax.ppermute(part_sums, 'col', ring))  6.84 us
    ppermute x3, starting transfers between devices, mirrored(): return lax.ppermute(value, ('row', 'col'), mirror)  2.8 us
  transfers between devices with their start and end apart: 6, of which 2 were waited for; matrix products, arithmetic and copies ran while one was open for 0% of the time, Pallas kernels for 21%

profile of v2, /device:TPU:0, one launch (start us, length us, event | category | flops | bytes accessed | tf_op | source)
XLA Modules:
  0.0 39.8 jit_solution(8876618810070833876)
XLA Ops:
  0.6 0.0 copy-start.2
  0.6 0.0 copy-start
  0.7 0.0 copy-start.3
  0.7 0.0 copy-start.4
  0.7 4.7 %shard_map.122 = (f32[2048,128]{1,0:T(8,128)S(1)}, s16[32,32,128]{2,1,0:T(8,128)(2,1)S(1)}, bf16[64,32,128]{2,1,0:T(8,128)(2,1)S(1)}, f32[128]{0:T(128)S(1)}, bf...) custom-call(bf16[64,64,128]{2,1,0:T(8,128)(2,1)} %pair_ref.1, f32[128]{0:T(128)} %gain_ref.2, ...), custom_call_target="tpu_custom_call" | custom-call | tf_op jit(solution)/shard_map/pallas_call | solution.py:28
  5.3 1.5 %collective-permute-start = (bf16[64,384]{1,0:T(8,128)(2,1)}, bf16[64,384]{1,0:T(8,128)(2,1)S(1)}, u32[]{:S(2)}, u32[]{:S(2)}) collective-permute-start(bf16[64,384]{1,0:T(8,128)(2,1)} %single_ref.1), channel_id=1, source_target_pairs={{0,0},{1,4},{2,8},{3,12},{4,1},{5,5},{6,9},{7,13},{8,2},{9,6},{10,... | collective-permute-start | bytes 147464 | tf_op jit(solution)/shard_map/ppermute | solution.py:327
  6.8 0.7 %collective-permute-start.2 = (s16[32,32,128]{2,1,0:T(8,128)(2,1)S(1)}, s16[32,32,128]{2,1,0:T(8,128)(2,1)S(1)}, u32[]{:S(2)}, u32[]{:S(2)}) collective-permute-start(s16[32,32,128]{2,1,0:T(8,128)(2,1)S(1)} %get-tuple-element.22), channel_id=1, source_target_pairs={{0,0},{1,4},{2,8},{3,12},{4,1},{5,5},{6,9},{7,13},{8,2},{9,6},{10,... | collective-permute-start | bytes 786440 | tf_op jit(solution)/shard_map/ppermute | solution.py:327
  7.5 0.0 copy-start.1
  7.5 3.1 %shard_map.123 = (f32[2048,128]{1,0:T(8,128)S(1)}, s16[32,32,128]{2,1,0:T(8,128)(2,1)S(1)}) custom-call(bf16[64,32,128]{2,1,0:T(8,128)(2,1)S(1)} %get-tuple-element.16.pair_ref, f32[128]{0:T(128)S(1)} %get-tuple-element.17.gain_ref, bf16[128,1024]{1,0:T(8,128)(2,1)S(1)} %get-tuple-element.18.in_ref, bf16[640,256]{1,0:T(8,128)(2,1)S(1)} %get-tuple-element.19.weight_ref), custom_call_target="tpu_custom_call" | custom-call | tf_op jit(solution)/shard_map/pallas_call | solution.py:28
  10.6 0.0 collective-permute-done.keys_ref
  10.6 0.7 %collective-permute-start.1 = (s16[32,32,128]{2,1,0:T(8,128)(2,1)S(1)}, s16[32,32,128]{2,1,0:T(8,128)(2,1)S(1)}, u32[]{:S(2)}, u32[]{:S(2)}) collective-permute-start(s16[32,32,128]{2,1,0:T(8,128)(2,1)S(1)} %get-tuple-element.24), channel_id=1, source_target_pairs={{0,0},{1,4},{2,8},{3,12},{4,1},{5,5},{6,9},{7,13},{8,2},{9,6},{10,... | collective-permute-start | bytes 786440 | tf_op jit(solution)/shard_map/ppermute | solution.py:327
  11.3 0.0 copy-done.2
  11.3 0.0 copy-done
  11.3 0.0 copy-done.3
  11.3 0.0 copy-done.4
  11.3 2.0 %shard_map.126 = (bf16[64,512]{1,0:T(8,128)(2,1)S(1)}, f32[64,384]{1,0:T(8,128)S(1)}) custom-call(bf16[64,384]{1,0:T(8,128)(2,1)S(1)} %copy-done.2, bf16[64,384]{1,0:T(8,128)(2,1)S(1)} %collective-permute-done.keys_ref, s32[64]{0:T(128)S(1)} %copy-done.4, f32[384]{0:T(512)S(1)} %copy-done.3, bf16[384,1536]{1,0:T(8,128)(2,1)S(1)} %copy-done, ...), custom_call_target="tpu_custom_call" | custom-call | tf_op jit(solution)/shard_map/pallas_call | solution.py:28
  13.3 13.7 %collective-permute-start.5 = (bf16[64,512]{1,0:T(8,128)(2,1)S(1)}, bf16[64,512]{1,0:T(8,128)(2,1)S(1)}, u32[]{:S(2)}, u32[]{:S(2)}) collective-permute-start(bf16[64,512]{1,0:T(8,128)(2,1)S(1)} %get-tuple-element.26.refs_0_), channel_id=1, source_target_pairs={{0,3},{1,0},{2,1},{3,2},{4,7},{5,4},{6,5},{7,6},{8,11},{9,8},{10,9... | collective-permute-start | bytes 196616 | tf_op jit(solution)/shard_map/ppermute | solution.py:375
  26.9 0.0 collective-permute-start.4
  26.9 0.2 collective-permute-start.3
  27.1 4.3 %collective-permute-done.5.refs_3_ = bf16[64,512]{1,0:T(8,128)(2,1)S(1)} collective-permute-done((bf16[64,512]{1,0:T(8,128)(2,1)S(1)}, bf16[64,512]{1,0:T(8,128)(2,1)S(1)}, u32[]{:S(2)}, u32[]{:S(2)}) %collective-permute-start.5) | collective-permute-done | bytes 65568 | tf_op jit(solution)/shard_map/ppermute | solution.py:375
  31.4 2.5 %collective-permute-done.4.refs_2_ = bf16[64,512]{1,0:T(8,128)(2,1)S(1)} collective-permute-done((bf16[64,512]{1,0:T(8,128)(2,1)S(1)}, bf16[64,512]{1,0:T(8,128)(2,1)S(1)}, u32[]{:S(2)}, u32[]{:S(2)}) %collective-permute-start.4) | collective-permute-done | bytes 65568 | tf_op jit(solution)/shard_map/ppermute | solution.py:375
  34.0 0.0 collective-permute-done.3.refs_1_
  34.0 0.0 copy-done.1
  34.0 1.0 %shard_map.127 = bf16[64,384]{1,0:T(8,128)(2,1)} custom-call(bf16[64,512]{1,0:T(8,128)(2,1)S(1)} %get-tuple-element.26.refs_0_, bf16[64,512]{1,0:T(8,128)(2,1)S(1)} %collective-permute-done.3.refs_1_, bf16[64,512]{1,0:T(8,128)(2,1)S(1)} %collective-permute-done.4.refs_2_, bf16[64,512]{1,0:T(8,128)(2,1)S(1)} %collective-permute-done.5.refs_3_, ...), custom_call_target="tpu_custom_call" | custom-call | tf_op jit(solution)/shard_map/pallas_call | solution.py:28
  35.0 0.0 collective-permute-done.2.code_ref
  35.0 2.4 %shard_map.124.refs_0_ = f32[64,64,64]{2,1,0:T(8,128)} custom-call(f32[2048,128]{1,0:T(8,128)S(1)} %get-tuple-element.15.first_ref, f32[2048,128]{1,0:T(8,128)S(1)} %get-tuple-element.20.second_ref, s16[32,32,128]{2,1,0:T(8,128)(2,1)S(1)} %collective-permute-done.2.code_ref), custom_call_target="tpu_custom_call" | custom-call | tf_op jit(solution)/shard_map/pallas_call | solution.py:28
  37.4 0.0 collective-permute-done.1.code_ref
  37.4 2.4 %shard_map.125 = f32[64,64,64]{2,1,0:T(8,128)} custom-call(f32[2048,128]{1,0:T(8,128)S(1)} %get-tuple-element.15.first_ref, f32[2048,128]{1,0:T(8,128)S(1)} %get-tuple-element.20.second_ref, s16[32,32,128]{2,1,0:T(8,128)(2,1)S(1)} %collective-permute-done.1.code_ref, f32[64,64,64]{2,1,0:T(8,128)} %shard_map.124.refs_0_), custom_call_target="tpu_custom_call", output_to_operand_aliasing={{}: (3, {})} | custom-call | tf_op jit(solution)/shard_map/pallas_call | solution.py:28
Async XLA Ops:
  0.6 10.6 %copy-start.2 = (bf16[64,384]{1,0:T(8,128)(2,1)S(1)}, bf16[64,384]{1,0:T(8,128)(2,1)}, u32[]{:S(2)}) copy-start(bf16[64,384]{1,0:T(8,128)(2,1)} %single_ref.1) | copy-start | bytes 147460
  0.6 10.6 %copy-start = (bf16[384,1536]{1,0:T(8,128)(2,1)S(1)}, bf16[384,1536]{1,0:T(8,128)(2,1)}, u32[]{:S(2)}) copy-start(bf16[384,1536]{1,0:T(8,128)(2,1)} %in_ref.3) | copy-start | bytes 3538948
  0.7 10.6 %copy-start.3 = (f32[384]{0:T(512)S(1)}, f32[384]{0:T(512)}, u32[]{:S(2)}) copy-start(f32[384]{0:T(512)} %gain_ref.3) | copy-start | bytes 4612
  0.7 10.6 %copy-start.4 = (s32[64]{0:T(128)S(1)}, s32[64]{0:T(128)}, u32[]{:S(2)}) copy-start(s32[64]{0:T(128)} %mask_ref.1) | copy-start | bytes 772
  5.3 5.2 %collective-permute-start = (bf16[64,384]{1,0:T(8,128)(2,1)}, bf16[64,384]{1,0:T(8,128)(2,1)S(1)}, u32[]{:S(2)}, u32[]{:S(2)}) collective-permute-start(bf16[64,384]{1,0:T(8,128)(2,1)} %single_ref.1), channel_id=1, source_target_pairs={{0,0},{1,4},{2,8},{3,12},{4,1},{5,5},{6,9},{7,13},{8,2},{9,6},{10,... | collective-permute-start | bytes 147464 | tf_op jit(solution)/shard_map/ppermute | solution.py:327
  6.8 28.2 %collective-permute-start.2 = (s16[32,32,128]{2,1,0:T(8,128)(2,1)S(1)}, s16[32,32,128]{2,1,0:T(8,128)(2,1)S(1)}, u32[]{:S(2)}, u32[]{:S(2)}) collective-permute-start(s16[32,32,128]{2,1,0:T(8,128)(2,1)S(1)} %get-tuple-element.22), channel_id=1, source_target_pairs={{0,0},{1,4},{2,8},{3,12},{4,1},{5,5},{6,9},{7,13},{8,2},{9,6},{10,... | collective-permute-start | bytes 786440 | tf_op jit(solution)/shard_map/ppermute | solution.py:327
  7.5 26.5 %copy-start.1 = (bf16[384,384]{1,0:T(8,128)(2,1)S(1)}, bf16[384,384]{1,0:T(8,128)(2,1)}, u32[]{:S(2)}) copy-start(bf16[384,384]{1,0:T(8,128)(2,1)} %refs_5_.1) | copy-start | bytes 884740
  10.6 26.8 %collective-permute-start.1 = (s16[32,32,128]{2,1,0:T(8,128)(2,1)S(1)}, s16[32,32,128]{2,1,0:T(8,128)(2,1)S(1)}, u32[]{:S(2)}, u32[]{:S(2)}) collective-permute-start(s16[32,32,128]{2,1,0:T(8,128)(2,1)S(1)} %get-tuple-element.24), channel_id=1, source_target_pairs={{0,0},{1,4},{2,8},{3,12},{4,1},{5,5},{6,9},{7,13},{8,2},{9,6},{10,... | collective-permute-start | bytes 786440 | tf_op jit(solution)/shard_map/ppermute | solution.py:327
  13.3 18.1 %collective-permute-start.5 = (bf16[64,512]{1,0:T(8,128)(2,1)S(1)}, bf16[64,512]{1,0:T(8,128)(2,1)S(1)}, u32[]{:S(2)}, u32[]{:S(2)}) collective-permute-start(bf16[64,512]{1,0:T(8,128)(2,1)S(1)} %get-tuple-element.26.refs_0_), channel_id=1, source_target_pairs={{0,3},{1,0},{2,1},{3,2},{4,7},{5,4},{6,5},{7,6},{8,11},{9,8},{10,9... | collective-permute-start | bytes 196616 | tf_op jit(solution)/shard_map/ppermute | solution.py:375
  26.9 7.0 %collective-permute-start.4 = (bf16[64,512]{1,0:T(8,128)(2,1)S(1)}, bf16[64,512]{1,0:T(8,128)(2,1)S(1)}, u32[]{:S(2)}, u32[]{:S(2)}) collective-permute-start(bf16[64,512]{1,0:T(8,128)(2,1)S(1)} %get-tuple-element.26.refs_0_), channel_id=1, source_target_pairs={{0,2},{1,3},{2,0},{3,1},{4,6},{5,7},{6,4},{7,5},{8,10},{9,11},{10,... | collective-permute-start | bytes 196616 | tf_op jit(solution)/shard_map/ppermute | solution.py:375
  26.9 7.0 %collective-permute-start.3 = (bf16[64,512]{1,0:T(8,128)(2,1)S(1)}, bf16[64,512]{1,0:T(8,128)(2,1)S(1)}, u32[]{:S(2)}, u32[]{:S(2)}) collective-permute-start(bf16[64,512]{1,0:T(8,128)(2,1)S(1)} %get-tuple-element.26.refs_0_), channel_id=1, source_target_pairs={{0,1},{1,2},{2,3},{3,0},{4,5},{5,6},{6,7},{7,4},{8,9},{9,10},{10,1... | collective-permute-start | bytes 196616 | tf_op jit(solution)/shard_map/ppermute | solution.py:375

commit v3 on v2

--- a/solution.py
+++ b/solution.py
@@ -12,7 +12,7 @@
 CODE_TOP = 32767.0
 PAIR_STEP = 8
 CODE_GROUP = 8
-SOFT_STEP = 8
+SOFT_STEP = 16
 VMEM_LIMIT = 56 * 1024 * 1024
 
 
@@ -323,8 +323,14 @@
         (r * col_count + c, c * col_count + r) for r in range(row_count) for c in range(col_count)
     ]
 
-    def mirrored(value):
-        return lax.ppermute(value, ("row", "col"), mirror)
+    key_pairs = [
+        (c * col_count + (r + col_count // 2) % col_count, r * col_count + c)
+        for r in range(row_count)
+        for c in range(col_count)
+    ]
+
+    def mirrored(value, pairs=mirror):
+        return lax.ppermute(value, ("row", "col"), pairs)
 
     bf16, f32, i16 = jnp.bfloat16, jnp.float32, jnp.int16
     heads_out = near((rows * half, LANES), f32)
@@ -351,7 +357,7 @@
     )
     received = [mirrored(code)]
     behind, _ = lax.optimization_barrier((single, code))
-    keys = mirrored(behind)
+    keys = mirrored(behind, key_pairs)
     second, code = call(
         functools.partial(second_kernel, bins),
         (heads_out, near((half, rows // 2, LANES), i16)),
@@ -373,12 +379,6 @@
     for away in range(1, col_count):
         ring = [(c, (c + away) % col_count) for c in range(col_count)]
         parts.append(lax.ppermute(part_sums, "col", ring))
-    single_update = call(
-        functools.partial(joined_kernel, heads, col_count),
-        jax.ShapeDtypeStruct((rows, width), bf16),
-        (*parts, gates, attention_out),
-        scratch=(pltpu.VMEM((rows, width), bf16), pltpu.SemaphoreType.DMA),
-    )
     distogram = None
     count = rows // 2
     for part in range(2):
@@ -393,6 +393,14 @@
             far=(3,) if part else (),
             aliases={3: 0} if part else {},
         )
+        if part == 0:
+            *parts, distogram = lax.optimization_barrier((*parts, distogram))
+            single_update = call(
+                functools.partial(joined_kernel, heads, col_count),
+                jax.ShapeDtypeStruct((rows, width), bf16),
+                (*parts, gates, attention_out),
+                scratch=(pltpu.VMEM((rows, width), bf16), pltpu.SemaphoreType.DMA),
+            )
     return (distogram, single_update)
 
 

time: 40.1 us -> 37.3 us (0.930)
  the two profiles are of different devices: /device:TPU:0 before, /device:TPU:21 now
where the time goes in v3:
time: 37.3 us; the launch traced here: 37.1 us
  Pallas kernels  14.4 us (39%)
  starting transfers between devices  11.6 us (31%)
  waiting for transfers between devices  10.3 us (28%)
  between operations  0.8 us (2%)
    pallas_call x6, Pallas kernels, call(): pl.pallas_call(kernel, out_shape=outs, in_specs=[pl.BlockSpec(memory_spac...  14.4 us
    ppermute x3, waiting for transfers between devices, mirrored(): return lax.ppermute(value, ('row', 'col'), pairs)  10.3 us
    ppermute x3, starting transfers between devices, mirrored(): return lax.ppermute(value, ('row', 'col'), pairs)  9.29 us
    ppermute x3, starting transfers between devices, body(): parts.append(lax.ppermute(part_sums, 'col', ring))  2.32 us
  transfers between devices with their start and end apart: 6, of which 2 were waited for; matrix products, arithmetic and copies ran while one was open for 0% of the time, Pallas kernels for 21%

profile of v3, /device:TPU:21, one launch (start us, length us, event | category | flops | bytes accessed | tf_op | source)
XLA Modules:
  0.0 37.1 jit_solution(14520681630684623871)
XLA Ops:
  0.6 0.0 copy-start.2
  0.6 0.0 copy-start
  0.7 0.0 copy-start.3
  0.7 0.0 copy-start.4
  0.7 4.6 %shard_map.122 = (f32[2048,128]{1,0:T(8,128)S(1)}, s16[32,32,128]{2,1,0:T(8,128)(2,1)S(1)}, bf16[64,32,128]{2,1,0:T(8,128)(2,1)S(1)}, f32[128]{0:T(128)S(1)}, bf...) custom-call(bf16[64,64,128]{2,1,0:T(8,128)(2,1)} %pair_ref.1, f32[128]{0:T(128)} %gain_ref.2, ...), custom_call_target="tpu_custom_call" | custom-call | tf_op jit(solution)/shard_map/pallas_call | solution.py:28
  5.3 2.8 %collective-permute-start = (bf16[64,384]{1,0:T(8,128)(2,1)}, bf16[64,384]{1,0:T(8,128)(2,1)S(1)}, u32[]{:S(2)}, u32[]{:S(2)}) collective-permute-start(bf16[64,384]{1,0:T(8,128)(2,1)} %single_ref.1), channel_id=1, source_target_pairs={{2,0},{6,1},{10,2},{14,3},{3,4},{7,5},{11,6},{15,7},{0,8},{4,9},{8... | collective-permute-start | bytes 147464 | tf_op jit(solution)/shard_map/ppermute | solution.py:333
  8.1 1.9 %collective-permute-start.5 = (s16[32,32,128]{2,1,0:T(8,128)(2,1)S(1)}, s16[32,32,128]{2,1,0:T(8,128)(2,1)S(1)}, u32[]{:S(2)}, u32[]{:S(2)}) collective-permute-start(s16[32,32,128]{2,1,0:T(8,128)(2,1)S(1)} %get-tuple-element.27), channel_id=1, source_target_pairs={{0,0},{1,4},{2,8},{3,12},{4,1},{5,5},{6,9},{7,13},{8,2},{9,6},{10,... | collective-permute-start | bytes 786440 | tf_op jit(solution)/shard_map/ppermute | solution.py:333
  10.1 3.0 %shard_map.123 = (f32[2048,128]{1,0:T(8,128)S(1)}, s16[32,32,128]{2,1,0:T(8,128)(2,1)S(1)}) custom-call(bf16[64,32,128]{2,1,0:T(8,128)(2,1)S(1)} %get-tuple-element.21.pair_ref, f32[128]{0:T(128)S(1)} %get-tuple-element.22.gain_ref, bf16[128,1024]{1,0:T(8,128)(2,1)S(1)} %get-tuple-element.23.in_ref, bf16[640,256]{1,0:T(8,128)(2,1)S(1)} %get-tuple-element.24.weight_ref), custom_call_target="tpu_custom_call" | custom-call | tf_op jit(solution)/shard_map/pallas_call | solution.py:28
  13.1 0.0 collective-permute-done.keys_ref
  13.1 4.5 %collective-permute-start.1 = (s16[32,32,128]{2,1,0:T(8,128)(2,1)S(1)}, s16[32,32,128]{2,1,0:T(8,128)(2,1)S(1)}, u32[]{:S(2)}, u32[]{:S(2)}) collective-permute-start(s16[32,32,128]{2,1,0:T(8,128)(2,1)S(1)} %get-tuple-element.29), channel_id=1, source_target_pairs={{0,0},{1,4},{2,8},{3,12},{4,1},{5,5},{6,9},{7,13},{8,2},{9,6},{10,... | collective-permute-start | bytes 786440 | tf_op jit(solution)/shard_map/ppermute | solution.py:333
  17.7 0.0 copy-done.2
  17.7 0.0 copy-done
  17.7 0.0 copy-done.3
  17.7 0.0 copy-done.4
  17.7 2.0 %shard_map.124 = (bf16[64,512]{1,0:T(8,128)(2,1)S(1)}, f32[64,384]{1,0:T(8,128)S(1)}) custom-call(bf16[64,384]{1,0:T(8,128)(2,1)S(1)} %copy-done.2, bf16[64,384]{1,0:T(8,128)(2,1)S(1)} %collective-permute-done.keys_ref, s32[64]{0:T(128)S(1)} %copy-done.4, f32[384]{0:T(512)S(1)} %copy-done.3, bf16[384,1536]{1,0:T(8,128)(2,1)S(1)} %copy-done, ...), custom_call_target="tpu_custom_call" | custom-call | tf_op jit(solution)/shard_map/pallas_call | solution.py:28
  19.7 0.0 copy-start.1
  19.7 0.6 %collective-permute-start.4 = (bf16[64,512]{1,0:T(8,128)(2,1)S(1)}, bf16[64,512]{1,0:T(8,128)(2,1)S(1)}, u32[]{:S(2)}, u32[]{:S(2)}) collective-permute-start(bf16[64,512]{1,0:T(8,128)(2,1)S(1)} %get-tuple-element.33.refs_0_), channel_id=1, source_target_pairs={{0,3},{1,0},{2,1},{3,2},{4,7},{5,4},{6,5},{7,6},{8,11},{9,8},{10,9... | collective-permute-start | bytes 196616 | tf_op jit(solution)/shard_map/ppermute | solution.py:381
  20.3 0.0 collective-permute-start.3
  20.3 1.7 %collective-permute-start.2 = (bf16[64,512]{1,0:T(8,128)(2,1)S(1)}, bf16[64,512]{1,0:T(8,128)(2,1)S(1)}, u32[]{:S(2)}, u32[]{:S(2)}) collective-permute-start(bf16[64,512]{1,0:T(8,128)(2,1)S(1)} %get-tuple-element.33.refs_0_), channel_id=1, source_target_pairs={{0,1},{1,2},{2,3},{3,0},{4,5},{5,6},{6,7},{7,4},{8,9},{9,10},{10,1... | collective-permute-start | bytes 196616 | tf_op jit(solution)/shard_map/ppermute | solution.py:381
  22.0 8.8 %collective-permute-done.5.code_ref = s16[32,32,128]{2,1,0:T(8,128)(2,1)S(1)} collective-permute-done((s16[32,32,128]{2,1,0:T(8,128)(2,1)S(1)}, s16[32,32,128]{2,1,0:T(8,128)(2,1)S(1)}, u32[]{:S(2)}, u32[]{:S(2)}) %collective-permute-start.5) | collective-permute-done | bytes 262176 | tf_op jit(solution)/shard_map/ppermute | solution.py:333
  30.8 1.9 %shard_map.125.refs_0_ = f32[64,64,64]{2,1,0:T(8,128)} custom-call(f32[2048,128]{1,0:T(8,128)S(1)} %get-tuple-element.20.first_ref, f32[2048,128]{1,0:T(8,128)S(1)} %get-tuple-element.25.second_ref, s16[32,32,128]{2,1,0:T(8,128)(2,1)S(1)} %collective-permute-done.5.code_ref), custom_call_target="tpu_custom_call" | custom-call | tf_op jit(solution)/shard_map/pallas_call | solution.py:28
  32.6 0.0 collective-permute-done.4.refs_3_
  32.6 0.0 collective-permute-done.3.refs_2_
  32.6 0.0 collective-permute-done.2.refs_1_
  32.7 0.0 copy-done.1
  32.7 1.1 %shard_map.127 = bf16[64,384]{1,0:T(8,128)(2,1)} custom-call(bf16[64,512]{1,0:T(8,128)(2,1)S(1)} %get-tuple-element.33.refs_0_, bf16[64,512]{1,0:T(8,128)(2,1)S(1)} %collective-permute-done.2.refs_1_, bf16[64,512]{1,0:T(8,128)(2,1)S(1)} %collective-permute-done.3.refs_2_, bf16[64,512]{1,0:T(8,128)(2,1)S(1)} %collective-permute-done.4.refs_3_, ...), custom_call_target="tpu_custom_call" | custom-call | tf_op jit(solution)/shard_map/pallas_call | solution.py:28
  33.7 1.6 %collective-permute-done.1.code_ref = s16[32,32,128]{2,1,0:T(8,128)(2,1)S(1)} collective-permute-done((s16[32,32,128]{2,1,0:T(8,128)(2,1)S(1)}, s16[32,32,128]{2,1,0:T(8,128)(2,1)S(1)}, u32[]{:S(2)}, u32[]{:S(2)}) %collective-permute-start.1) | collective-permute-done | bytes 262176 | tf_op jit(solution)/shard_map/ppermute | solution.py:333
  35.3 1.9 %shard_map.126 = f32[64,64,64]{2,1,0:T(8,128)} custom-call(f32[2048,128]{1,0:T(8,128)S(1)} %get-tuple-element.20.first_ref, f32[2048,128]{1,0:T(8,128)S(1)} %get-tuple-element.25.second_ref, s16[32,32,128]{2,1,0:T(8,128)(2,1)S(1)} %collective-permute-done.1.code_ref, f32[64,64,64]{2,1,0:T(8,128)} %shard_map.125.refs_0_), custom_call_target="tpu_custom_call", output_to_operand_aliasing={{}: (3, {})} | custom-call | tf_op jit(solution)/shard_map/pallas_call | solution.py:28
Async XLA Ops:
  0.6 17.0 %copy-start.2 = (bf16[64,384]{1,0:T(8,128)(2,1)S(1)}, bf16[64,384]{1,0:T(8,128)(2,1)}, u32[]{:S(2)}) copy-start(bf16[64,384]{1,0:T(8,128)(2,1)} %single_ref.1) | copy-start | bytes 147460
  0.6 17.0 %copy-start = (bf16[384,1536]{1,0:T(8,128)(2,1)S(1)}, bf16[384,1536]{1,0:T(8,128)(2,1)}, u32[]{:S(2)}) copy-start(bf16[384,1536]{1,0:T(8,128)(2,1)} %in_ref.3) | copy-start | bytes 3538948
  0.7 17.0 %copy-start.3 = (f32[384]{0:T(512)S(1)}, f32[384]{0:T(512)}, u32[]{:S(2)}) copy-start(f32[384]{0:T(512)} %gain_ref.3) | copy-start | bytes 4612
  0.7 17.0 %copy-start.4 = (s32[64]{0:T(128)S(1)}, s32[64]{0:T(128)}, u32[]{:S(2)}) copy-start(s32[64]{0:T(128)} %mask_ref.1) | copy-start | bytes 772
  5.3 7.8 %collective-permute-start = (bf16[64,384]{1,0:T(8,128)(2,1)}, bf16[64,384]{1,0:T(8,128)(2,1)S(1)}, u32[]{:S(2)}, u32[]{:S(2)}) collective-permute-start(bf16[64,384]{1,0:T(8,128)(2,1)} %single_ref.1), channel_id=1, source_target_pairs={{2,0},{6,1},{10,2},{14,3},{3,4},{7,5},{11,6},{15,7},{0,8},{4,9},{8... | collective-permute-start | bytes 147464 | tf_op jit(solution)/shard_map/ppermute | solution.py:333
  8.1 22.6 %collective-permute-start.5 = (s16[32,32,128]{2,1,0:T(8,128)(2,1)S(1)}, s16[32,32,128]{2,1,0:T(8,128)(2,1)S(1)}, u32[]{:S(2)}, u32[]{:S(2)}) collective-permute-start(s16[32,32,128]{2,1,0:T(8,128)(2,1)S(1)} %get-tuple-element.27), channel_id=1, source_target_pairs={{0,0},{1,4},{2,8},{3,12},{4,1},{5,5},{6,9},{7,13},{8,2},{9,6},{10,... | collective-permute-start | bytes 786440 | tf_op jit(solution)/shard_map/ppermute | solution.py:333
  13.1 22.2 %collective-permute-start.1 = (s16[32,32,128]{2,1,0:T(8,128)(2,1)S(1)}, s16[32,32,128]{2,1,0:T(8,128)(2,1)S(1)}, u32[]{:S(2)}, u32[]{:S(2)}) collective-permute-start(s16[32,32,128]{2,1,0:T(8,128)(2,1)S(1)} %get-tuple-element.29), channel_id=1, source_target_pairs={{0,0},{1,4},{2,8},{3,12},{4,1},{5,5},{6,9},{7,13},{8,2},{9,6},{10,... | collective-permute-start | bytes 786440 | tf_op jit(solution)/shard_map/ppermute | solution.py:333
  19.7 13.0 %copy-start.1 = (bf16[384,384]{1,0:T(8,128)(2,1)S(1)}, bf16[384,384]{1,0:T(8,128)(2,1)}, u32[]{:S(2)}) copy-start(bf16[384,384]{1,0:T(8,128)(2,1)} %refs_5_.1) | copy-start | bytes 884740
  19.7 13.0 %collective-permute-start.4 = (bf16[64,512]{1,0:T(8,128)(2,1)S(1)}, bf16[64,512]{1,0:T(8,128)(2,1)S(1)}, u32[]{:S(2)}, u32[]{:S(2)}) collective-permute-start(bf16[64,512]{1,0:T(8,128)(2,1)S(1)} %get-tuple-element.33.refs_0_), channel_id=1, source_target_pairs={{0,3},{1,0},{2,1},{3,2},{4,7},{5,4},{6,5},{7,6},{8,11},{9,8},{10,9... | collective-permute-start | bytes 196616 | tf_op jit(solution)/shard_map/ppermute | solution.py:381
  20.3 12.4 %collective-permute-start.3 = (bf16[64,512]{1,0:T(8,128)(2,1)S(1)}, bf16[64,512]{1,0:T(8,128)(2,1)S(1)}, u32[]{:S(2)}, u32[]{:S(2)}) collective-permute-start(bf16[64,512]{1,0:T(8,128)(2,1)S(1)} %get-tuple-element.33.refs_0_), channel_id=1, source_target_pairs={{0,2},{1,3},{2,0},{3,1},{4,6},{5,7},{6,4},{7,5},{8,10},{9,11},{10,... | collective-permute-start | bytes 196616 | tf_op jit(solution)/shard_map/ppermute | solution.py:381
  20.3 12.4 %collective-permute-start.2 = (bf16[64,512]{1,0:T(8,128)(2,1)S(1)}, bf16[64,512]{1,0:T(8,128)(2,1)S(1)}, u32[]{:S(2)}, u32[]{:S(2)}) collective-permute-start(bf16[64,512]{1,0:T(8,128)(2,1)S(1)} %get-tuple-element.33.refs_0_), channel_id=1, source_target_pairs={{0,1},{1,2},{2,3},{3,0},{4,5},{5,6},{6,7},{7,4},{8,9},{9,10},{10,1... | collective-permute-start | bytes 196616 | tf_op jit(solution)/shard_map/ppermute | solution.py:381

commit v4 on v2

--- a/solution.py
+++ b/solution.py
@@ -12,7 +12,7 @@
 CODE_TOP = 32767.0
 PAIR_STEP = 8
 CODE_GROUP = 8
-SOFT_STEP = 8
+SOFT_STEP = 16
 VMEM_LIMIT = 56 * 1024 * 1024
 
 
@@ -180,39 +180,65 @@
     fill_code(bins, rows, cols, heads_ref, code_ref)
 
 
-def softmax_kernel(part, step, first_ref, second_ref, code_ref, *refs):
-    out_ref, held, sems = refs[-3:]
+def apart(size):
+    return size // 2
+
+
+def softmax_kernel(part, turn, step, size, heads, first_ref, second_ref, code_ref, *refs):
+    if turn == 2:
+        parts, (gates_ref, weight_ref, _) = refs[:size], refs[size : size + 3]
+        out_ref, single_ref, held, sems, single_held, single_sem = refs[size + 3 :]
+    else:
+        out_ref, held, sems = refs[-3:]
     rows, cols, bins = held.shape
     half = cols // 2
+    distance = lax.axis_index("col") - lax.axis_index("row")
+    relayed = (distance == apart(size)) | (distance == apart(size) - size)
     lanes = lane_index((step * half, LANES))
     low = lanes < bins
-    copies = []
-    for start in range(0, rows, step):
-        code = code_ref[start : start + step].reshape(step * half, LANES)
-        code = code.astype(jnp.int32).astype(jnp.float32)
-        power = jnp.sum(jnp.where(lanes == bins - 1, code, 0.0), axis=1, keepdims=True)
-        other = code * (jnp.exp2(power) * (1.0 / CODE_TOP))
-        other = jnp.where(lanes % bins == bins - 1, 0.0, other)
-        at = pl.ds((part * rows + start) * half, step * half)
-        for side, own_ref in enumerate((first_ref, second_ref)):
-            mirrored = other if side == 0 else pltpu.roll(other, bins, 1)
-            logits = jnp.where(low, own_ref[at, :] + mirrored, -jnp.inf)
-            top = jnp.max(logits, axis=1, keepdims=True)
-            raised = jnp.exp(logits - top)
-            share = raised * (1.0 / jnp.sum(raised, axis=1, keepdims=True))
-            held[start : start + step, side * half : (side + 1) * half, :] = share[
-                :, :bins
-            ].reshape(step, half, bins)
-        copies.append(
-            pltpu.make_async_copy(
-                held.at[pl.ds(start, step)],
-                out_ref.at[pl.ds(part * rows + start, step)],
-                sems.at[start // step],
+
+    def work():
+        copies = []
+        for start in range(0, rows, step):
+            code = code_ref[start : start + step]
+            if turn == 0:
+                code = lax.select_n(distance == 0, code, refs[0][start : start + step])
+            code = code.reshape(step * half, LANES)
+            code = code.astype(jnp.int32).astype(jnp.float32)
+            power = jnp.sum(jnp.where(lanes == bins - 1, code, 0.0), axis=1, keepdims=True)
+            other = code * (jnp.exp2(power) * (1.0 / CODE_TOP))
+            other = jnp.where(lanes % bins == bins - 1, 0.0, other)
+            at = pl.ds((part * rows + start) * half, step * half)
+            for side, own_ref in enumerate((first_ref, second_ref)):
+                mirrored = other if side == 0 else pltpu.roll(other, bins, 1)
+                logits = jnp.where(low, own_ref[at, :] + mirrored, -jnp.inf)
+                top = jnp.max(logits, axis=1, keepdims=True)
+                raised = jnp.exp(logits - top)
+                share = raised * (1.0 / jnp.sum(raised, axis=1, keepdims=True))
+                held[start : start + step, side * half : (side + 1) * half, :] = share[
+                    :, :bins
+                ].reshape(step, half, bins)
+            copies.append(
+                pltpu.make_async_copy(
+                    held.at[pl.ds(start, step)],
+                    out_ref.at[pl.ds(part * rows + start, step)],
+                    sems.at[start // step],
+                )
             )
-        )
-        copies[-1].start()
-    for copy in copies:
-        copy.wait()
+            copies[-1].start()
+        for copy in copies:
+            copy.wait()
+
+    if turn == 2:
+        single_held[...] = joined(heads, parts, gates_ref, weight_ref)
+        single_copy = pltpu.make_async_copy(single_held, single_ref, single_sem)
+        single_copy.start()
+    if turn == 1:
+        work()
+    else:
+        pl.when(relayed if turn == 2 else jnp.logical_not(relayed))(work)
+    if turn == 2:
+        single_copy.wait()
 
 
 def attention_kernel(
@@ -274,8 +300,7 @@
     part_ref[:, width:] = jnp.sum(spread, axis=1).astype(jnp.bfloat16)
 
 
-def joined_kernel(heads, count, *refs):
-    parts, (gates_ref, out_weight_ref, out_ref, held, sem) = refs[:count], refs[count:]
+def joined(heads, parts, gates_ref, out_weight_ref):
     width = gates_ref.shape[1]
     head_width = width // heads
     shape = (LANES, width)
@@ -293,10 +318,7 @@
         total += factor
         summed += factor * part[:, :width].astype(jnp.float32)
     gated = (gates_ref[...] * (summed / total)).astype(jnp.bfloat16)
-    held[...] = dot(gated, out_weight_ref[...]).astype(jnp.bfloat16)
-    copy = pltpu.make_async_copy(held, out_ref, sem)
-    copy.start()
-    copy.wait()
+    return dot(gated, out_weight_ref[...]).astype(jnp.bfloat16)
 
 
 def body(
@@ -319,13 +341,18 @@
     heads, bins = bias_weight.shape[1], bin_weight.shape[1]
     hidden = transition_out.shape[0]
     half = cols // 2
-    mirror = [
-        (r * col_count + c, c * col_count + r) for r in range(row_count) for c in range(col_count)
-    ]
-
-    def mirrored(value):
-        return lax.ppermute(value, ("row", "col"), mirror)
-
+    grid = [(r, c) for r in range(row_count) for c in range(col_count)]
+    far = [(r, c) for r, c in grid if c == (r + apart(col_count)) % col_count]
+
+    def moved(value, pairs):
+        pairs = [(a * col_count + b, c * col_count + d) for (a, b), (c, d) in pairs]
+        return lax.ppermute(value, ("row", "col"), pairs)
+
+    mirror = [((r, c), (c, r)) for r, c in grid]
+    near_mirror = [((r, c), (c, r)) for r, c in grid if r != c and (r, c) not in far]
+    to_relay = [((r, c), (r, r)) for r, c in far]
+    from_relay = [((r, r), (c, r)) for r, c in far]
+    half_way = [((c, (r + apart(col_count)) % col_count), (r, c)) for r, c in grid]
     bf16, f32, i16 = jnp.bfloat16, jnp.float32, jnp.int16
     heads_out = near((rows * half, LANES), f32)
     first, code, later, *kept = call(
@@ -349,9 +376,9 @@
         ),
         far=range(6),
     )
-    received = [mirrored(code)]
+    own_code, early = code, moved(code, near_mirror + to_relay)
     behind, _ = lax.optimization_barrier((single, code))
-    keys = mirrored(behind)
+    keys = moved(behind, half_way)
     second, code = call(
         functools.partial(second_kernel, bins),
         (heads_out, near((half, rows // 2, LANES), i16)),
@@ -359,7 +386,8 @@
     )
     own = (first, second)
     code, keys = lax.optimization_barrier((code, keys))
-    received.append(mirrored(code))
+    direct = moved(code, mirror)
+    relayed = moved(early, from_relay)
     part_sums, gates = call(
         functools.partial(attention_kernel, bins),
         (
@@ -373,26 +401,32 @@
     for away in range(1, col_count):
         ring = [(c, (c + away) % col_count) for c in range(col_count)]
         parts.append(lax.ppermute(part_sums, "col", ring))
-    single_update = call(
-        functools.partial(joined_kernel, heads, col_count),
-        jax.ShapeDtypeStruct((rows, width), bf16),
-        (*parts, gates, attention_out),
-        scratch=(pltpu.VMEM((rows, width), bf16), pltpu.SemaphoreType.DMA),
-    )
-    distogram = None
     count = rows // 2
-    for part in range(2):
-        distogram = call(
-            functools.partial(softmax_kernel, part, SOFT_STEP),
-            jax.ShapeDtypeStruct((rows, cols, bins), jnp.float32),
-            (*own, received[part]) + ((distogram,) if part else ()),
-            scratch=(
-                pltpu.VMEM((count, cols, bins), jnp.float32),
-                pltpu.SemaphoreType.DMA((count // SOFT_STEP,)),
-            ),
-            far=(3,) if part else (),
-            aliases={3: 0} if part else {},
+    distogram_out = jax.ShapeDtypeStruct((rows, cols, bins), f32)
+    single_out = jax.ShapeDtypeStruct((rows, width), bf16)
+    scratch = (pltpu.VMEM((count, cols, bins), f32), pltpu.SemaphoreType.DMA((count // SOFT_STEP,)))
+
+    def turn(number, part, codes, outs, more=(), scratch=scratch):
+        last = 2 + len(codes) + len(more) - 1
+        return call(
+            functools.partial(softmax_kernel, part, number, SOFT_STEP, col_count, heads),
+            outs,
+            (*own, *codes, *more),
+            scratch=scratch,
+            far=(last,) if number else (),
+            aliases={last: 0} if number else {},
         )
+
+    distogram = turn(0, 0, (early, own_code), distogram_out)
+    distogram = turn(1, 1, (direct,), distogram_out, (distogram,))
+    distogram, single_update = turn(
+        2,
+        0,
+        (relayed,),
+        (distogram_out, single_out),
+        (*parts, gates, attention_out, distogram),
+        scratch=(*scratch, pltpu.VMEM((rows, width), bf16), pltpu.SemaphoreType.DMA),
+    )
     return (distogram, single_update)
 
 

time: 40.1 us -> 35.6 us (0.89)
  the two profiles are of different devices: /device:TPU:0 before, /device:TPU:29 now
where the time goes in v4:
time: 35.6 us; the launch traced here: 35.4 us
  Pallas kernels  13.8 us (39%)
  starting transfers between devices  11.4 us (32%)
  waiting for transfers between devices  9.43 us (26%)
  between operations  0.82 us (2%)
    pallas_call x6, Pallas kernels, call(): pl.pallas_call(kernel, out_shape=outs, in_specs=[pl.BlockSpec(memory_spac...  13.8 us
    ppermute x4, waiting for transfers between devices, moved(): return lax.ppermute(value, ('row', 'col'), pairs)  9.42 us
    ppermute x4, starting transfers between devices, moved(): return lax.ppermute(value, ('row', 'col'), pairs)  6.39 us
    ppermute x3, starting transfers between devices, body(): parts.append(lax.ppermute(part_sums, 'col', ring))  5.01 us
  transfers between devices with their start and end apart: 7, of which 2 were waited for; matrix products, arithmetic and copies ran while one was open for 0% of the time, Pallas kernels for 19%

profile of v4, /device:TPU:29, one launch (start us, length us, event | category | flops | bytes accessed | tf_op | source)
XLA Modules:
  0.0 35.4 jit_solution(17508737226435172889)
XLA Ops:
  0.6 0.0 copy-start.2
  0.6 0.0 copy-start.4
  0.7 0.0 copy-start.3
  0.7 0.0 copy-start
  0.7 4.6 %shard_map.122 = (f32[2048,128]{1,0:T(8,128)S(1)}, s16[32,32,128]{2,1,0:T(8,128)(2,1)S(1)}, bf16[64,32,128]{2,1,0:T(8,128)(2,1)S(1)}, f32[128]{0:T(128)S(1)}, bf...) custom-call(bf16[64,64,128]{2,1,0:T(8,128)(2,1)} %pair_ref.1, f32[128]{0:T(128)} %gain_ref.2, ...), custom_call_target="tpu_custom_call" | custom-call | tf_op jit(solution)/shard_map/pallas_call | solution.py:28
  5.3 3.1 %collective-permute-start = (s16[32,32,128]{2,1,0:T(8,128)(2,1)S(1)}, s16[32,32,128]{2,1,0:T(8,128)(2,1)S(1)}, u32[]{:S(2)}, u32[]{:S(2)}) collective-permute-start(s16[32,32,128]{2,1,0:T(8,128)(2,1)S(1)} %get-tuple-element.21.refs_0_), channel_id=1, source_target_pairs={{1,4},{3,12},{4,1},{6,9},{9,6},{11,14},{12,3},{14,11},{2,0},{7,5},... | collective-permute-start | bytes 786440 | tf_op jit(solution)/shard_map/ppermute | solution.py:349
  8.4 0.1 collective-permute-start.2
  8.5 3.0 %shard_map.123 = (f32[2048,128]{1,0:T(8,128)S(1)}, s16[32,32,128]{2,1,0:T(8,128)(2,1)S(1)}) custom-call(bf16[64,32,128]{2,1,0:T(8,128)(2,1)S(1)} %get-tuple-element.16.pair_ref, f32[128]{0:T(128)S(1)} %get-tuple-element.17.gain_ref, bf16[128,1024]{1,0:T(8,128)(2,1)S(1)} %get-tuple-element.18.in_ref, bf16[640,256]{1,0:T(8,128)(2,1)S(1)} %get-tuple-element.19.weight_ref), custom_call_target="tpu_custom_call" | custom-call | tf_op jit(solution)/shard_map/pallas_call | solution.py:28
  11.5 2.9 %collective-permute-done.2.keys_ref = bf16[64,384]{1,0:T(8,128)(2,1)S(1)} collective-permute-done((bf16[64,384]{1,0:T(8,128)(2,1)}, bf16[64,384]{1,0:T(8,128)(2,1)S(1)}, u32[]{:S(2)}, u32[]{:S(2)}) %collective-permute-start.2) | collective-permute-done | bytes 49184 | tf_op jit(solution)/shard_map/ppermute | solution.py:349
  14.4 1.9 %collective-permute-start.6 = (s16[32,32,128]{2,1,0:T(8,128)(2,1)S(1)}, s16[32,32,128]{2,1,0:T(8,128)(2,1)S(1)}, u32[]{:S(2)}, u32[]{:S(2)}) collective-permute-start(s16[32,32,128]{2,1,0:T(8,128)(2,1)S(1)} %get-tuple-element.27), channel_id=1, source_target_pairs={{0,0},{1,4},{2,8},{3,12},{4,1},{5,5},{6,9},{7,13},{8,2},{9,6},{10,... | collective-permute-start | bytes 786440 | tf_op jit(solution)/shard_map/ppermute | solution.py:349
  16.3 0.0 collective-permute-done.code_ref
  16.3 1.3 %collective-permute-start.1 = (s16[32,32,128]{2,1,0:T(8,128)(2,1)S(1)}, s16[32,32,128]{2,1,0:T(8,128)(2,1)S(1)}, u32[]{:S(2)}, u32[]{:S(2)}) collective-permute-start(s16[32,32,128]{2,1,0:T(8,128)(2,1)S(1)} %collective-permute-done.code_ref), channel_id=1, source_target_pairs={{0,8},{5,13},{10,2},{15,7},{16,24},{21,29},{26,18},{31,23}} | collective-permute-start | bytes 786440 | tf_op jit(solution)/shard_map/ppermute | solution.py:349
  17.6 0.0 copy-done.2
  17.7 0.0 copy-done.4
  17.7 0.0 copy-done.3
  17.7 0.0 copy-done
  17.7 2.0 %shard_map.124 = (bf16[64,512]{1,0:T(8,128)(2,1)S(1)}, f32[64,384]{1,0:T(8,128)S(1)}) custom-call(bf16[64,384]{1,0:T(8,128)(2,1)S(1)} %copy-done.2, bf16[64,384]{1,0:T(8,128)(2,1)S(1)} %collective-permute-done.2.keys_ref, s32[64]{0:T(128)S(1)} %copy-done.4, f32[384]{0:T(512)S(1)} %copy-done.3, bf16[384,1536]{1,0:T(8,128)(2,1)S(1)} %copy-done, ...), custom_call_target="tpu_custom_call" | custom-call | tf_op jit(solution)/shard_map/pallas_call | solution.py:28
  19.6 1.0 %collective-permute-start.3 = (bf16[64,512]{1,0:T(8,128)(2,1)S(1)}, bf16[64,512]{1,0:T(8,128)(2,1)S(1)}, u32[]{:S(2)}, u32[]{:S(2)}) collective-permute-start(bf16[64,512]{1,0:T(8,128)(2,1)S(1)} %get-tuple-element.25.refs_0_), channel_id=1, source_target_pairs={{0,1},{1,2},{2,3},{3,0},{4,5},{5,6},{6,7},{7,4},{8,9},{9,10},{10,1... | collective-permute-start | bytes 196616 | tf_op jit(solution)/shard_map/ppermute | solution.py:403
  20.7 3.3 %collective-permute-start.4 = (bf16[64,512]{1,0:T(8,128)(2,1)S(1)}, bf16[64,512]{1,0:T(8,128)(2,1)S(1)}, u32[]{:S(2)}, u32[]{:S(2)}) collective-permute-start(bf16[64,512]{1,0:T(8,128)(2,1)S(1)} %get-tuple-element.25.refs_0_), channel_id=1, source_target_pairs={{0,2},{1,3},{2,0},{3,1},{4,6},{5,7},{6,4},{7,5},{8,10},{9,11},{10,... | collective-permute-start | bytes 196616 | tf_op jit(solution)/shard_map/ppermute | solution.py:403
  23.9 0.7 %collective-permute-start.5 = (bf16[64,512]{1,0:T(8,128)(2,1)S(1)}, bf16[64,512]{1,0:T(8,128)(2,1)S(1)}, u32[]{:S(2)}, u32[]{:S(2)}) collective-permute-start(bf16[64,512]{1,0:T(8,128)(2,1)S(1)} %get-tuple-element.25.refs_0_), channel_id=1, source_target_pairs={{0,3},{1,0},{2,1},{3,2},{4,7},{5,4},{6,5},{7,6},{8,11},{9,8},{10,9... | collective-permute-start | bytes 196616 | tf_op jit(solution)/shard_map/ppermute | solution.py:403
  24.7 0.0 copy-start.1
  24.7 6.5 %collective-permute-done.6.code_ref = s16[32,32,128]{2,1,0:T(8,128)(2,1)S(1)} collective-permute-done((s16[32,32,128]{2,1,0:T(8,128)(2,1)S(1)}, s16[32,32,128]{2,1,0:T(8,128)(2,1)S(1)}, u32[]{:S(2)}, u32[]{:S(2)}) %collective-permute-start.6) | collective-permute-done | bytes 262176 | tf_op jit(solution)/shard_map/ppermute | solution.py:349
  31.2 1.9 %shard_map.126.refs_6_ = f32[64,64,64]{2,1,0:T(8,128)} custom-call(f32[2048,128]{1,0:T(8,128)S(1)} %get-tuple-element.15.first_ref, f32[2048,128]{1,0:T(8,128)S(1)} %get-tuple-element.20.second_ref, s16[32,32,128]{2,1,0:T(8,128)(2,1)S(1)} %collective-permute-done.6.code_ref, f32[64,64,64]{2,1,0:T(8,128)} %shard_map.125.refs_0_), custom_call_target="tpu_custom_call", output_to_operand_aliasing={{}: (3, {})} | custom-call | tf_op jit(solution)/shard_map/pallas_call | solution.py:28
  33.1 0.0 collective-permute-done.3.refs_1_
  33.1 0.0 collective-permute-done.4.refs_2_
  33.1 0.0 collective-permute-done.5.refs_3_
  33.1 0.0 collective-permute-done.1.code_ref
  33.1 0.0 copy-done.1
  33.2 2.3 %shard_map.127 = (f32[64,64,64]{2,1,0:T(8,128)}, bf16[64,384]{1,0:T(8,128)(2,1)}) custom-call(f32[2048,128]{1,0:T(8,128)S(1)} %get-tuple-element.15.first_ref, f32[2048,128]{1,0:T(8,128)S(1)} %get-tuple-element.20.second_ref, s16[32,32,128]{2,1,0:T(8,128)(2,1)S(1)} %collective-permute-done.1.code_ref, ...), custom_call_target="tpu_custom_call", output_to_operand_aliasing={{0}: (9, {})} | custom-call | tf_op jit(solution)/shard_map/pallas_call | solution.py:28
  (1 shorter events, 0.0 us)
Async XLA Ops:
  0.6 17.0 %copy-start.2 = (bf16[64,384]{1,0:T(8,128)(2,1)S(1)}, bf16[64,384]{1,0:T(8,128)(2,1)}, u32[]{:S(2)}) copy-start(bf16[64,384]{1,0:T(8,128)(2,1)} %single_ref.1) | copy-start | bytes 147460
  0.6 17.0 %copy-start.4 = (s32[64]{0:T(128)S(1)}, s32[64]{0:T(128)}, u32[]{:S(2)}) copy-start(s32[64]{0:T(128)} %mask_ref.1) | copy-start | bytes 772
  0.7 17.0 %copy-start.3 = (f32[384]{0:T(512)S(1)}, f32[384]{0:T(512)}, u32[]{:S(2)}) copy-start(f32[384]{0:T(512)} %gain_ref.3) | copy-start | bytes 4612
  0.7 17.0 %copy-start = (bf16[384,1536]{1,0:T(8,128)(2,1)S(1)}, bf16[384,1536]{1,0:T(8,128)(2,1)}, u32[]{:S(2)}) copy-start(bf16[384,1536]{1,0:T(8,128)(2,1)} %in_ref.3) | copy-start | bytes 3538948
  5.3 11.0 %collective-permute-start = (s16[32,32,128]{2,1,0:T(8,128)(2,1)S(1)}, s16[32,32,128]{2,1,0:T(8,128)(2,1)S(1)}, u32[]{:S(2)}, u32[]{:S(2)}) collective-permute-start(s16[32,32,128]{2,1,0:T(8,128)(2,1)S(1)} %get-tuple-element.21.refs_0_), channel_id=1, source_target_pairs={{1,4},{3,12},{4,1},{6,9},{9,6},{11,14},{12,3},{14,11},{2,0},{7,5},... | collective-permute-start | bytes 786440 | tf_op jit(solution)/shard_map/ppermute | solution.py:349
  8.4 6.0 %collective-permute-start.2 = (bf16[64,384]{1,0:T(8,128)(2,1)}, bf16[64,384]{1,0:T(8,128)(2,1)S(1)}, u32[]{:S(2)}, u32[]{:S(2)}) collective-permute-start(bf16[64,384]{1,0:T(8,128)(2,1)} %single_ref.1), channel_id=1, source_target_pairs={{2,0},{6,1},{10,2},{14,3},{3,4},{7,5},{11,6},{15,7},{0,8},{4,9},{8... | collective-permute-start | bytes 147464 | tf_op jit(solution)/shard_map/ppermute | solution.py:349
  14.4 16.8 %collective-permute-start.6 = (s16[32,32,128]{2,1,0:T(8,128)(2,1)S(1)}, s16[32,32,128]{2,1,0:T(8,128)(2,1)S(1)}, u32[]{:S(2)}, u32[]{:S(2)}) collective-permute-start(s16[32,32,128]{2,1,0:T(8,128)(2,1)S(1)} %get-tuple-element.27), channel_id=1, source_target_pairs={{0,0},{1,4},{2,8},{3,12},{4,1},{5,5},{6,9},{7,13},{8,2},{9,6},{10,... | collective-permute-start | bytes 786440 | tf_op jit(solution)/shard_map/ppermute | solution.py:349
  16.3 16.8 %collective-permute-start.1 = (s16[32,32,128]{2,1,0:T(8,128)(2,1)S(1)}, s16[32,32,128]{2,1,0:T(8,128)(2,1)S(1)}, u32[]{:S(2)}, u32[]{:S(2)}) collective-permute-start(s16[32,32,128]{2,1,0:T(8,128)(2,1)S(1)} %collective-permute-done.code_ref), channel_id=1, source_target_pairs={{0,8},{5,13},{10,2},{15,7},{16,24},{21,29},{26,18},{31,23}} | collective-permute-start | bytes 786440 | tf_op jit(solution)/shard_map/ppermute | solution.py:349
  19.6 13.5 %collective-permute-start.3 = (bf16[64,512]{1,0:T(8,128)(2,1)S(1)}, bf16[64,512]{1,0:T(8,128)(2,1)S(1)}, u32[]{:S(2)}, u32[]{:S(2)}) collective-permute-start(bf16[64,512]{1,0:T(8,128)(2,1)S(1)} %get-tuple-element.25.refs_0_), channel_id=1, source_target_pairs={{0,1},{1,2},{2,3},{3,0},{4,5},{5,6},{6,7},{7,4},{8,9},{9,10},{10,1... | collective-permute-start | bytes 196616 | tf_op jit(solution)/shard_map/ppermute | solution.py:403
  20.7 12.5 %collective-permute-start.4 = (bf16[64,512]{1,0:T(8,128)(2,1)S(1)}, bf16[64,512]{1,0:T(8,128)(2,1)S(1)}, u32[]{:S(2)}, u32[]{:S(2)}) collective-permute-start(bf16[64,512]{1,0:T(8,128)(2,1)S(1)} %get-tuple-element.25.refs_0_), channel_id=1, source_target_pairs={{0,2},{1,3},{2,0},{3,1},{4,6},{5,7},{6,4},{7,5},{8,10},{9,11},{10,... | collective-permute-start | bytes 196616 | tf_op jit(solution)/shard_map/ppermute | solution.py:403
  23.9 9.2 %collective-permute-start.5 = (bf16[64,512]{1,0:T(8,128)(2,1)S(1)}, bf16[64,512]{1,0:T(8,128)(2,1)S(1)}, u32[]{:S(2)}, u32[]{:S(2)}) collective-permute-start(bf16[64,512]{1,0:T(8,128)(2,1)S(1)} %get-tuple-element.25.refs_0_), channel_id=1, source_target_pairs={{0,3},{1,0},{2,1},{3,2},{4,7},{5,4},{6,5},{7,6},{8,11},{9,8},{10,9... | collective-permute-start | bytes 196616 | tf_op jit(solution)/shard_map/ppermute | solution.py:403
  24.7 8.5 %copy-start.1 = (bf16[384,384]{1,0:T(8,128)(2,1)S(1)}, bf16[384,384]{1,0:T(8,128)(2,1)}, u32[]{:S(2)}) copy-start(bf16[384,384]{1,0:T(8,128)(2,1)} %refs_5_.1) | copy-start | bytes 884740

commit v5 on v4

--- a/solution.py
+++ b/solution.py
@@ -13,6 +13,7 @@
 PAIR_STEP = 8
 CODE_GROUP = 8
 SOFT_STEP = 16
+ROW_TILE = 8
 VMEM_LIMIT = 56 * 1024 * 1024
 
 
@@ -160,7 +161,7 @@
     gain_copy = bring(gain_ref, gain_near, sems.at[3])
     tile_copy = bring(pair_ref.at[:, pl.ds(0, cols)], tile, sems.at[4])
     in_copy = bring(in_ref, in_near, sems.at[5])
-    later = bring(pair_ref.at[:, pl.ds(cols, cols)], later_ref, sems.at[6])
+    later = bring(pair_ref.at[:, pl.ds(cols, later_ref.shape[1])], later_ref, sems.at[6])
     for copy in small:
         copy.wait()
     fill_weights(out_near, bias_near, bin_near, flat_weight, weight_ref)
@@ -184,7 +185,7 @@
     return size // 2
 
 
-def softmax_kernel(part, turn, step, size, heads, first_ref, second_ref, code_ref, *refs):
+def softmax_kernel(part, turn, most, size, heads, first_ref, second_ref, code_ref, *refs):
     if turn == 2:
         parts, (gates_ref, weight_ref, _) = refs[:size], refs[size : size + 3]
         out_ref, single_ref, held, sems, single_held, single_sem = refs[size + 3 :]
@@ -194,12 +195,24 @@
     half = cols // 2
     distance = lax.axis_index("col") - lax.axis_index("row")
     relayed = (distance == apart(size)) | (distance == apart(size) - size)
-    lanes = lane_index((step * half, LANES))
-    low = lanes < bins
+    begin = first_ref.shape[1] if part else 0
+
+    def own(side, at):
+        cut = first_ref.shape[1]
+        low, high = side * half, (side + 1) * half
+        pieces = []
+        if low < cut:
+            pieces.append(first_ref[at, low : min(high, cut)])
+        if high > cut:
+            pieces.append(second_ref[at, max(low - cut, 0) : high - cut])
+        return jnp.concatenate(pieces, axis=1).reshape(-1, LANES)
 
     def work():
         copies = []
-        for start in range(0, rows, step):
+        for start in range(0, rows, most):
+            step = min(most, rows - start)
+            lanes = lane_index((step * half, LANES))
+            low = lanes < bins
             code = code_ref[start : start + step]
             if turn == 0:
                 code = lax.select_n(distance == 0, code, refs[0][start : start + step])
@@ -208,10 +221,10 @@
             power = jnp.sum(jnp.where(lanes == bins - 1, code, 0.0), axis=1, keepdims=True)
             other = code * (jnp.exp2(power) * (1.0 / CODE_TOP))
             other = jnp.where(lanes % bins == bins - 1, 0.0, other)
-            at = pl.ds((part * rows + start) * half, step * half)
-            for side, own_ref in enumerate((first_ref, second_ref)):
+            at = slice(begin + start, begin + start + step)
+            for side in range(2):
                 mirrored = other if side == 0 else pltpu.roll(other, bins, 1)
-                logits = jnp.where(low, own_ref[at, :] + mirrored, -jnp.inf)
+                logits = jnp.where(low, own(side, at) + mirrored, -jnp.inf)
                 top = jnp.max(logits, axis=1, keepdims=True)
                 raised = jnp.exp(logits - top)
                 share = raised * (1.0 / jnp.sum(raised, axis=1, keepdims=True))
@@ -221,8 +234,8 @@
             copies.append(
                 pltpu.make_async_copy(
                     held.at[pl.ds(start, step)],
-                    out_ref.at[pl.ds(part * rows + start, step)],
-                    sems.at[start // step],
+                    out_ref.at[pl.ds(begin + start, step)],
+                    sems.at[start // most],
                 )
             )
             copies[-1].start()
@@ -257,7 +270,6 @@
     rows, width = single_ref.shape
     heads, cols = scores.shape[1:]
     head_width = width // heads
-    half = cols // 2
     gain = gain_ref[...].reshape(1, -1)
     query_inner = (centered(single_ref[...].astype(jnp.float32)) * gain).astype(jnp.bfloat16)
     key_inner = (centered(keys_ref[...].astype(jnp.float32)) * gain).astype(jnp.bfloat16)
@@ -276,7 +288,7 @@
     pick = (lane == lax.broadcasted_iota(jnp.int32, shape, 0) + bins).astype(jnp.bfloat16)
     for row in range(rows):
         block = jnp.concatenate(
-            [ref[row * half : (row + 1) * half, :] for ref in (first_ref, second_ref)], axis=0
+            [first_ref[row], second_ref[row]], axis=0
         )
         scores[row] += dot_t(pick, jnp.concatenate(split(block), axis=1))
     kept = jnp.where(mask_ref[...].reshape(1, -1) > 0, scores[...].reshape(rows * heads, cols), -1000000000.0)
@@ -340,7 +352,8 @@
     width = single.shape[1]
     heads, bins = bias_weight.shape[1], bin_weight.shape[1]
     hidden = transition_out.shape[0]
-    half = cols // 2
+    cut = cols * 5 // 8 // ROW_TILE * ROW_TILE
+    rest = cols - cut
     grid = [(r, c) for r in range(row_count) for c in range(col_count)]
     far = [(r, c) for r, c in grid if c == (r + apart(col_count)) % col_count]
 
@@ -354,20 +367,19 @@
     from_relay = [((r, r), (c, r)) for r, c in far]
     half_way = [((c, (r + apart(col_count)) % col_count), (r, c)) for r, c in grid]
     bf16, f32, i16 = jnp.bfloat16, jnp.float32, jnp.int16
-    heads_out = near((rows * half, LANES), f32)
     first, code, later, *kept = call(
         first_kernel,
         (
-            heads_out,
-            near((half, rows // 2, LANES), i16),
-            near((rows, half, channels), bf16),
+            near((rows * cut, LANES), f32),
+            near((cut, rows // 2, LANES), i16),
+            near((rows, rest, channels), bf16),
             near(pair_gain.shape, f32),
             near(transition_in.shape, bf16),
             near((hidden + channels, 2 * LANES), bf16),
         ),
         (pair, pair_gain, transition_in, transition_out, bias_weight.T, bin_weight.T),
         scratch=(
-            pltpu.VMEM((rows, half, channels), bf16),
+            pltpu.VMEM((rows, cut, channels), bf16),
             pltpu.VMEM(transition_out.shape, bf16),
             pltpu.VMEM((heads, channels), f32),
             pltpu.VMEM((bins, channels), f32),
@@ -381,13 +393,14 @@
     keys = moved(behind, half_way)
     second, code = call(
         functools.partial(second_kernel, bins),
-        (heads_out, near((half, rows // 2, LANES), i16)),
+        (near((rows * rest, LANES), f32), near((rest, rows // 2, LANES), i16)),
         (later, *kept),
     )
-    own = (first, second)
+    own = (first.reshape(rows, cut, LANES), second.reshape(rows, rest, LANES))
     code, keys = lax.optimization_barrier((code, keys))
     direct = moved(code, mirror)
-    relayed = moved(early, from_relay)
+    passed, _ = lax.optimization_barrier((early, code))
+    relayed = moved(passed, from_relay)
     part_sums, gates = call(
         functools.partial(attention_kernel, bins),
         (
@@ -401,12 +414,17 @@
     for away in range(1, col_count):
         ring = [(c, (c + away) % col_count) for c in range(col_count)]
         parts.append(lax.ppermute(part_sums, "col", ring))
-    count = rows // 2
     distogram_out = jax.ShapeDtypeStruct((rows, cols, bins), f32)
     single_out = jax.ShapeDtypeStruct((rows, width), bf16)
-    scratch = (pltpu.VMEM((count, cols, bins), f32), pltpu.SemaphoreType.DMA((count // SOFT_STEP,)))
-
-    def turn(number, part, codes, outs, more=(), scratch=scratch):
+
+    def turn(number, part, codes, outs, more=(), scratch=()):
+        count = codes[0].shape[0]
+        blocks = -(-count // SOFT_STEP)
+        scratch = (
+            pltpu.VMEM((count, cols, bins), f32),
+            pltpu.SemaphoreType.DMA((blocks,)),
+            *scratch,
+        )
         last = 2 + len(codes) + len(more) - 1
         return call(
             functools.partial(softmax_kernel, part, number, SOFT_STEP, col_count, heads),
@@ -425,7 +443,7 @@
         (relayed,),
         (distogram_out, single_out),
         (*parts, gates, attention_out, distogram),
-        scratch=(*scratch, pltpu.VMEM((rows, width), bf16), pltpu.SemaphoreType.DMA),
+        scratch=(pltpu.VMEM((rows, width), bf16), pltpu.SemaphoreType.DMA),
     )
     return (distogram, single_update)
 

time: 35.6 us -> 34.5 us (0.969)
  the two profiles are of different devices: /device:TPU:29 before, /device:TPU:15 now
where the time goes in v5:
time: 34.5 us; the launch traced here: 34.3 us
  starting transfers between devices  13.8 us (40%)
  Pallas kernels  13.6 us (39%)
  waiting for transfers between devices  6.06 us (18%)
  between operations  0.79 us (2%)
    pallas_call x6, Pallas kernels, call(): pl.pallas_call(kernel, out_shape=outs, in_specs=[pl.BlockSpec(memory_spac...  13.6 us
    ppermute x4, starting transfers between devices, moved(): return lax.ppermute(value, ('row', 'col'), pairs)  9.14 us
    ppermute x3, starting transfers between devices, body(): parts.append(lax.ppermute(part_sums, 'col', ring))  4.68 us
    ppermute x3, waiting for transfers between devices, body(): parts.append(lax.ppermute(part_sums, 'col', ring))  3.78 us
    ppermute x4, waiting for transfers between devices, moved(): return lax.ppermute(value, ('row', 'col'), pairs)  2.28 us
  transfers between devices with their start and end apart: 7, of which 3 were waited for; matrix products, arithmetic and copies ran while one was open for 0% of the time, Pallas kernels for 17%

profile of v5, /device:TPU:15, one launch (start us, length us, event | category | flops | bytes accessed | tf_op | source)
XLA Modules:
  0.0 34.3 jit_solution(6658742092875931398)
XLA Ops:
  0.6 0.0 copy-start.2
  0.6 0.0 copy-start.4
  0.7 0.0 copy-start.3
  0.7 0.0 copy-start
  0.7 5.0 %shard_map.122 = (f32[2560,128]{1,0:T(8,128)S(1)}, s16[40,32,128]{2,1,0:T(8,128)(2,1)S(1)}, bf16[64,24,128]{2,1,0:T(8,128)(2,1)S(1)}, f32[128]{0:T(128)S(1)}, bf...) custom-call(bf16[64,64,128]{2,1,0:T(8,128)(2,1)} %pair_ref.1, f32[128]{0:T(128)} %gain_ref.2, ...), custom_call_target="tpu_custom_call" | custom-call | tf_op jit(solution)/shard_map/pallas_call | solution.py:29
  5.7 2.2 %collective-permute-start = (s16[40,32,128]{2,1,0:T(8,128)(2,1)S(1)}, s16[40,32,128]{2,1,0:T(8,128)(2,1)S(1)}, u32[]{:S(2)}, u32[]{:S(2)}) collective-permute-start(s16[40,32,128]{2,1,0:T(8,128)(2,1)S(1)} %get-tuple-element.22.refs_0_), channel_id=1, source_target_pairs={{1,4},{3,12},{4,1},{6,9},{9,6},{11,14},{12,3},{14,11},{2,0},{7,5},... | collective-permute-start | bytes 983048 | tf_op jit(solution)/shard_map/ppermute | solution.py:362
  7.9 0.1 collective-permute-start.1
  8.0 2.3 %shard_map.123 = (f32[1536,128]{1,0:T(8,128)S(1)}, s16[24,32,128]{2,1,0:T(8,128)(2,1)S(1)}) custom-call(bf16[64,24,128]{2,1,0:T(8,128)(2,1)S(1)} %get-tuple-element.17.pair_ref, f32[128]{0:T(128)S(1)} %get-tuple-element.18.gain_ref, bf16[128,1024]{1,0:T(8,128)(2,1)S(1)} %get-tuple-element.19.in_ref, bf16[640,256]{1,0:T(8,128)(2,1)S(1)} %get-tuple-element.20.weight_ref), custom_call_target="tpu_custom_call" | custom-call | tf_op jit(solution)/shard_map/pallas_call | solution.py:29
  10.3 2.3 %collective-permute-done.1.keys_ref = bf16[64,384]{1,0:T(8,128)(2,1)S(1)} collective-permute-done((bf16[64,384]{1,0:T(8,128)(2,1)}, bf16[64,384]{1,0:T(8,128)(2,1)S(1)}, u32[]{:S(2)}, u32[]{:S(2)}) %collective-permute-start.1) | collective-permute-done | bytes 49184 | tf_op jit(solution)/shard_map/ppermute | solution.py:362
  12.6 0.0 collective-permute-done.code_ref
  12.6 1.3 %collective-permute-start.2 = (s16[40,32,128]{2,1,0:T(8,128)(2,1)S(1)}, s16[40,32,128]{2,1,0:T(8,128)(2,1)S(1)}, u32[]{:S(2)}, u32[]{:S(2)}) collective-permute-start(s16[40,32,128]{2,1,0:T(8,128)(2,1)S(1)} %collective-permute-done.code_ref), channel_id=1, source_target_pairs={{0,8},{5,13},{10,2},{15,7},{16,24},{21,29},{26,18},{31,23}} | collective-permute-start | bytes 983048 | tf_op jit(solution)/shard_map/ppermute | solution.py:362
  13.9 5.6 %collective-permute-start.6 = (s16[24,32,128]{2,1,0:T(8,128)(2,1)S(1)}, s16[24,32,128]{2,1,0:T(8,128)(2,1)S(1)}, u32[]{:S(2)}, u32[]{:S(2)}) collective-permute-start(s16[24,32,128]{2,1,0:T(8,128)(2,1)S(1)} %get-tuple-element.25), channel_id=1, source_target_pairs={{0,0},{1,4},{2,8},{3,12},{4,1},{5,5},{6,9},{7,13},{8,2},{9,6},{10,... | collective-permute-start | bytes 589832 | tf_op jit(solution)/shard_map/ppermute | solution.py:362
  19.5 0.0 copy-done.2
  19.5 0.0 copy-done.4
  19.5 0.0 copy-done.3
  19.5 0.0 copy-done
  19.5 2.0 %shard_map.124 = (bf16[64,512]{1,0:T(8,128)(2,1)S(1)}, f32[64,384]{1,0:T(8,128)S(1)}) custom-call(bf16[64,384]{1,0:T(8,128)(2,1)S(1)} %copy-done.2, bf16[64,384]{1,0:T(8,128)(2,1)S(1)} %collective-permute-done.1.keys_ref, s32[64]{0:T(128)S(1)} %copy-done.4, f32[384]{0:T(512)S(1)} %copy-done.3, bf16[384,1536]{1,0:T(8,128)(2,1)S(1)} %copy-done, ...), custom_call_target="tpu_custom_call" | custom-call | tf_op jit(solution)/shard_map/pallas_call | solution.py:29
  21.5 1.6 %collective-permute-start.3 = (bf16[64,512]{1,0:T(8,128)(2,1)S(1)}, bf16[64,512]{1,0:T(8,128)(2,1)S(1)}, u32[]{:S(2)}, u32[]{:S(2)}) collective-permute-start(bf16[64,512]{1,0:T(8,128)(2,1)S(1)} %get-tuple-element.28.refs_0_), channel_id=1, source_target_pairs={{0,1},{1,2},{2,3},{3,0},{4,5},{5,6},{6,7},{7,4},{8,9},{9,10},{10,1... | collective-permute-start | bytes 196616 | tf_op jit(solution)/shard_map/ppermute | solution.py:416
  23.1 3.1 %collective-permute-start.4 = (bf16[64,512]{1,0:T(8,128)(2,1)S(1)}, bf16[64,512]{1,0:T(8,128)(2,1)S(1)}, u32[]{:S(2)}, u32[]{:S(2)}) collective-permute-start(bf16[64,512]{1,0:T(8,128)(2,1)S(1)} %get-tuple-element.28.refs_0_), channel_id=1, source_target_pairs={{0,2},{1,3},{2,0},{3,1},{4,6},{5,7},{6,4},{7,5},{8,10},{9,11},{10,... | collective-permute-start | bytes 196616 | tf_op jit(solution)/shard_map/ppermute | solution.py:416
  26.2 0.0 collective-permute-start.5
  26.2 0.0 copy-start.1
  26.2 0.0 collective-permute-done.6.code_ref
  26.3 1.7 %shard_map.126.refs_6_ = f32[64,64,64]{2,1,0:T(8,128)} custom-call(f32[64,40,128]{2,1,0:T(8,128)S(1)} %bitcast.6, f32[64,24,128]{2,1,0:T(8,128)S(1)} %bitcast.10, s16[24,32,128]{2,1,0:T(8,128)(2,1)S(1)} %collective-permute-done.6.code_ref, f32[64,64,64]{2,1,0:T(8,128)} %shard_map.125.refs_0_), custom_call_target="tpu_custom_call", output_to_operand_aliasing={{}: (3, {})} | custom-call | tf_op jit(solution)/shard_map/pallas_call | solution.py:29
  27.9 0.0 collective-permute-done.3.refs_1_
  27.9 3.7 %collective-permute-done.4.refs_2_ = bf16[64,512]{1,0:T(8,128)(2,1)S(1)} collective-permute-done((bf16[64,512]{1,0:T(8,128)(2,1)S(1)}, bf16[64,512]{1,0:T(8,128)(2,1)S(1)}, u32[]{:S(2)}, u32[]{:S(2)}) %collective-permute-start.4) | collective-permute-done | bytes 65568 | tf_op jit(solution)/shard_map/ppermute | solution.py:416
  31.7 0.1 collective-permute-done.5.refs_3_
  31.7 0.0 collective-permute-done.2.code_ref
  31.7 0.0 copy-done.1
  31.7 2.6 %shard_map.127 = (f32[64,64,64]{2,1,0:T(8,128)}, bf16[64,384]{1,0:T(8,128)(2,1)}) custom-call(f32[64,40,128]{2,1,0:T(8,128)S(1)} %bitcast.7, f32[64,24,128]{2,1,0:T(8,128)S(1)} %bitcast.11, s16[40,32,128]{2,1,0:T(8,128)(2,1)S(1)} %collective-permute-done.2.code_ref, bf16[64,512]{1,0:T(8,128)(2,1)S(1)} %get-tuple-element.28.refs_0_, ...), custom_call_target="tpu_custom_call", output_to_operand_aliasing={{0}: (9, {})} | custom-call | tf_op jit(solution)/shard_map/pallas_call | solution.py:29
  (1 shorter events, 0.0 us)
Async XLA Ops:
  0.6 18.9 %copy-start.2 = (bf16[64,384]{1,0:T(8,128)(2,1)S(1)}, bf16[64,384]{1,0:T(8,128)(2,1)}, u32[]{:S(2)}) copy-start(bf16[64,384]{1,0:T(8,128)(2,1)} %single_ref.1) | copy-start | bytes 147460
  0.6 18.9 %copy-start.4 = (s32[64]{0:T(128)S(1)}, s32[64]{0:T(128)}, u32[]{:S(2)}) copy-start(s32[64]{0:T(128)} %mask_ref.1) | copy-start | bytes 772
  0.7 18.9 %copy-start.3 = (f32[384]{0:T(512)S(1)}, f32[384]{0:T(512)}, u32[]{:S(2)}) copy-start(f32[384]{0:T(512)} %gain_ref.3) | copy-start | bytes 4612
  0.7 18.9 %copy-start = (bf16[384,1536]{1,0:T(8,128)(2,1)S(1)}, bf16[384,1536]{1,0:T(8,128)(2,1)}, u32[]{:S(2)}) copy-start(bf16[384,1536]{1,0:T(8,128)(2,1)} %in_ref.3) | copy-start | bytes 3538948
  5.7 6.9 %collective-permute-start = (s16[40,32,128]{2,1,0:T(8,128)(2,1)S(1)}, s16[40,32,128]{2,1,0:T(8,128)(2,1)S(1)}, u32[]{:S(2)}, u32[]{:S(2)}) collective-permute-start(s16[40,32,128]{2,1,0:T(8,128)(2,1)S(1)} %get-tuple-element.22.refs_0_), channel_id=1, source_target_pairs={{1,4},{3,12},{4,1},{6,9},{9,6},{11,14},{12,3},{14,11},{2,0},{7,5},... | collective-permute-start | bytes 983048 | tf_op jit(solution)/shard_map/ppermute | solution.py:362
  7.9 4.7 %collective-permute-start.1 = (bf16[64,384]{1,0:T(8,128)(2,1)}, bf16[64,384]{1,0:T(8,128)(2,1)S(1)}, u32[]{:S(2)}, u32[]{:S(2)}) collective-permute-start(bf16[64,384]{1,0:T(8,128)(2,1)} %single_ref.1), channel_id=1, source_target_pairs={{2,0},{6,1},{10,2},{14,3},{3,4},{7,5},{11,6},{15,7},{0,8},{4,9},{8... | collective-permute-start | bytes 147464 | tf_op jit(solution)/shard_map/ppermute | solution.py:362
  12.6 19.1 %collective-permute-start.2 = (s16[40,32,128]{2,1,0:T(8,128)(2,1)S(1)}, s16[40,32,128]{2,1,0:T(8,128)(2,1)S(1)}, u32[]{:S(2)}, u32[]{:S(2)}) collective-permute-start(s16[40,32,128]{2,1,0:T(8,128)(2,1)S(1)} %collective-permute-done.code_ref), channel_id=1, source_target_pairs={{0,8},{5,13},{10,2},{15,7},{16,24},{21,29},{26,18},{31,23}} | collective-permute-start | bytes 983048 | tf_op jit(solution)/shard_map/ppermute | solution.py:362
  13.9 12.4 %collective-permute-start.6 = (s16[24,32,128]{2,1,0:T(8,128)(2,1)S(1)}, s16[24,32,128]{2,1,0:T(8,128)(2,1)S(1)}, u32[]{:S(2)}, u32[]{:S(2)}) collective-permute-start(s16[24,32,128]{2,1,0:T(8,128)(2,1)S(1)} %get-tuple-element.25), channel_id=1, source_target_pairs={{0,0},{1,4},{2,8},{3,12},{4,1},{5,5},{6,9},{7,13},{8,2},{9,6},{10,... | collective-permute-start | bytes 589832 | tf_op jit(solution)/shard_map/ppermute | solution.py:362
  21.5 6.4 %collective-permute-start.3 = (bf16[64,512]{1,0:T(8,128)(2,1)S(1)}, bf16[64,512]{1,0:T(8,128)(2,1)S(1)}, u32[]{:S(2)}, u32[]{:S(2)}) collective-permute-start(bf16[64,512]{1,0:T(8,128)(2,1)S(1)} %get-tuple-element.28.refs_0_), channel_id=1, source_target_pairs={{0,1},{1,2},{2,3},{3,0},{4,5},{5,6},{6,7},{7,4},{8,9},{9,10},{10,1... | collective-permute-start | bytes 196616 | tf_op jit(solution)/shard_map/ppermute | solution.py:416
  23.1 8.6 %collective-permute-start.4 = (bf16[64,512]{1,0:T(8,128)(2,1)S(1)}, bf16[64,512]{1,0:T(8,128)(2,1)S(1)}, u32[]{:S(2)}, u32[]{:S(2)}) collective-permute-start(bf16[64,512]{1,0:T(8,128)(2,1)S(1)} %get-tuple-element.28.refs_0_), channel_id=1, source_target_pairs={{0,2},{1,3},{2,0},{3,1},{4,6},{5,7},{6,4},{7,5},{8,10},{9,11},{10,... | collective-permute-start | bytes 196616 | tf_op jit(solution)/shard_map/ppermute | solution.py:416
  26.2 5.5 %collective-permute-start.5 = (bf16[64,512]{1,0:T(8,128)(2,1)S(1)}, bf16[64,512]{1,0:T(8,128)(2,1)S(1)}, u32[]{:S(2)}, u32[]{:S(2)}) collective-permute-start(bf16[64,512]{1,0:T(8,128)(2,1)S(1)} %get-tuple-element.28.refs_0_), channel_id=1, source_target_pairs={{0,3},{1,0},{2,1},{3,2},{4,7},{5,4},{6,5},{7,6},{8,11},{9,8},{10,9... | collective-permute-start | bytes 196616 | tf_op jit(solution)/shard_map/ppermute | solution.py:416
  26.2 5.5 %copy-start.1 = (bf16[384,384]{1,0:T(8,128)(2,1)S(1)}, bf16[384,384]{1,0:T(8,128)(2,1)}, u32[]{:S(2)}) copy-start(bf16[384,384]{1,0:T(8,128)(2,1)} %refs_5_.1) | copy-start | bytes 884740

commit v6 on v5

--- a/solution.py
+++ b/solution.py
@@ -333,6 +333,10 @@
     return dot(gated, out_weight_ref[...]).astype(jnp.bfloat16)
 
 
+def partner(place, away, size):
+    return place ^ away if size & (size - 1) == 0 else (place + away) % size
+
+
 def body(
     row_count,
     col_count,
@@ -411,8 +415,8 @@
         scratch=(pltpu.VMEM((rows, heads, cols), jnp.float32),),
     )
     parts = [part_sums]
-    for away in range(1, col_count):
-        ring = [(c, (c + away) % col_count) for c in range(col_count)]
+    for away in [*range(2, col_count), 1]:
+        ring = [(c, partner(c, away, col_count)) for c in range(col_count)]
         parts.append(lax.ppermute(part_sums, "col", ring))
     distogram_out = jax.ShapeDtypeStruct((rows, cols, bins), f32)
     single_out = jax.ShapeDtypeStruct((rows, width), bf16)

time: 34.5 us -> 34.3 us (level)
  the two profiles are of different devices: /device:TPU:15 before, /device:TPU:20 now
where the time goes in v6:
time: 34.3 us; the launch traced here: 34.1 us
  Pallas kernels  13.6 us (40%)
  starting transfers between devices  12.5 us (36%)
  waiting for transfers between devices  7.13 us (21%)
  between operations  0.8 us (2%)
    pallas_call x6, Pallas kernels, call(): pl.pallas_call(kernel, out_shape=outs, in_specs=[pl.BlockSpec(memory_spac...  13.6 us
    ppermute x4, starting transfers between devices, moved(): return lax.ppermute(value, ('row', 'col'), pairs)  7.04 us
    ppermute x3, starting transfers between devices, body(): parts.append(lax.ppermute(part_sums, 'col', ring))  5.47 us
    ppermute x3, waiting for transfers between devices, body(): parts.append(lax.ppermute(part_sums, 'col', ring))  3.68 us
    ppermute x4, waiting for transfers between devices, moved(): return lax.ppermute(value, ('row', 'col'), pairs)  3.45 us
  transfers between devices with their start and end apart: 7, of which 2 were waited for; matrix products, arithmetic and copies ran while one was open for 0% of the time, Pallas kernels for 17%

profile of v6, /device:TPU:20, one launch (start us, length us, event | category | flops | bytes accessed | tf_op | source)
XLA Modules:
  0.0 34.1 jit_solution(17606098440942909679)
XLA Ops:
  0.6 0.0 copy-start.2
  0.6 0.0 copy-start.4
  0.7 0.0 copy-start.3
  0.7 0.0 copy-start
  0.7 5.0 %shard_map.122 = (f32[2560,128]{1,0:T(8,128)S(1)}, s16[40,32,128]{2,1,0:T(8,128)(2,1)S(1)}, bf16[64,24,128]{2,1,0:T(8,128)(2,1)S(1)}, f32[128]{0:T(128)S(1)}, bf...) custom-call(bf16[64,64,128]{2,1,0:T(8,128)(2,1)} %pair_ref.1, f32[128]{0:T(128)} %gain_ref.2, ...), custom_call_target="tpu_custom_call" | custom-call | tf_op jit(solution)/shard_map/pallas_call | solution.py:29
  5.7 3.4 %collective-permute-start = (s16[40,32,128]{2,1,0:T(8,128)(2,1)S(1)}, s16[40,32,128]{2,1,0:T(8,128)(2,1)S(1)}, u32[]{:S(2)}, u32[]{:S(2)}) collective-permute-start(s16[40,32,128]{2,1,0:T(8,128)(2,1)S(1)} %get-tuple-element.22.refs_0_), channel_id=1, source_target_pairs={{1,4},{3,12},{4,1},{6,9},{9,6},{11,14},{12,3},{14,11},{2,0},{7,5},... | collective-permute-start | bytes 983048 | tf_op jit(solution)/shard_map/ppermute | solution.py:366
  9.2 0.1 collective-permute-start.1
  9.2 2.3 %shard_map.123 = (f32[1536,128]{1,0:T(8,128)S(1)}, s16[24,32,128]{2,1,0:T(8,128)(2,1)S(1)}) custom-call(bf16[64,24,128]{2,1,0:T(8,128)(2,1)S(1)} %get-tuple-element.17.pair_ref, f32[128]{0:T(128)S(1)} %get-tuple-element.18.gain_ref, bf16[128,1024]{1,0:T(8,128)(2,1)S(1)} %get-tuple-element.19.in_ref, bf16[640,256]{1,0:T(8,128)(2,1)S(1)} %get-tuple-element.20.weight_ref), custom_call_target="tpu_custom_call" | custom-call | tf_op jit(solution)/shard_map/pallas_call | solution.py:29
  11.5 3.4 %collective-permute-done.1.keys_ref = bf16[64,384]{1,0:T(8,128)(2,1)S(1)} collective-permute-done((bf16[64,384]{1,0:T(8,128)(2,1)}, bf16[64,384]{1,0:T(8,128)(2,1)S(1)}, u32[]{:S(2)}, u32[]{:S(2)}) %collective-permute-start.1) | collective-permute-done | bytes 49184 | tf_op jit(solution)/shard_map/ppermute | solution.py:366
  15.0 0.0 collective-permute-done.code_ref
  15.0 1.3 %collective-permute-start.2 = (s16[40,32,128]{2,1,0:T(8,128)(2,1)S(1)}, s16[40,32,128]{2,1,0:T(8,128)(2,1)S(1)}, u32[]{:S(2)}, u32[]{:S(2)}) collective-permute-start(s16[40,32,128]{2,1,0:T(8,128)(2,1)S(1)} %collective-permute-done.code_ref), channel_id=1, source_target_pairs={{0,8},{5,13},{10,2},{15,7},{16,24},{21,29},{26,18},{31,23}} | collective-permute-start | bytes 983048 | tf_op jit(solution)/shard_map/ppermute | solution.py:366
  16.3 2.3 %collective-permute-start.6 = (s16[24,32,128]{2,1,0:T(8,128)(2,1)S(1)}, s16[24,32,128]{2,1,0:T(8,128)(2,1)S(1)}, u32[]{:S(2)}, u32[]{:S(2)}) collective-permute-start(s16[24,32,128]{2,1,0:T(8,128)(2,1)S(1)} %get-tuple-element.25), channel_id=1, source_target_pairs={{0,0},{1,4},{2,8},{3,12},{4,1},{5,5},{6,9},{7,13},{8,2},{9,6},{10,... | collective-permute-start | bytes 589832 | tf_op jit(solution)/shard_map/ppermute | solution.py:366
  18.6 0.0 copy-done.2
  18.6 0.0 copy-done.4
  18.6 0.0 copy-done.3
  18.6 0.0 copy-done
  18.6 1.9 %shard_map.124 = (bf16[64,512]{1,0:T(8,128)(2,1)S(1)}, f32[64,384]{1,0:T(8,128)S(1)}) custom-call(bf16[64,384]{1,0:T(8,128)(2,1)S(1)} %copy-done.2, bf16[64,384]{1,0:T(8,128)(2,1)S(1)} %collective-permute-done.1.keys_ref, s32[64]{0:T(128)S(1)} %copy-done.4, f32[384]{0:T(512)S(1)} %copy-done.3, bf16[384,1536]{1,0:T(8,128)(2,1)S(1)} %copy-done, ...), custom_call_target="tpu_custom_call" | custom-call | tf_op jit(solution)/shard_map/pallas_call | solution.py:29
  20.6 0.7 %collective-permute-start.3 = (bf16[64,512]{1,0:T(8,128)(2,1)S(1)}, bf16[64,512]{1,0:T(8,128)(2,1)S(1)}, u32[]{:S(2)}, u32[]{:S(2)}) collective-permute-start(bf16[64,512]{1,0:T(8,128)(2,1)S(1)} %get-tuple-element.28.refs_0_), channel_id=1, source_target_pairs={{0,2},{1,3},{2,0},{3,1},{4,6},{5,7},{6,4},{7,5},{8,10},{9,11},{10,... | collective-permute-start | bytes 196616 | tf_op jit(solution)/shard_map/ppermute | solution.py:420
  21.3 4.7 %collective-permute-start.4 = (bf16[64,512]{1,0:T(8,128)(2,1)S(1)}, bf16[64,512]{1,0:T(8,128)(2,1)S(1)}, u32[]{:S(2)}, u32[]{:S(2)}) collective-permute-start(bf16[64,512]{1,0:T(8,128)(2,1)S(1)} %get-tuple-element.28.refs_0_), channel_id=1, source_target_pairs={{0,3},{1,2},{2,1},{3,0},{4,7},{5,6},{6,5},{7,4},{8,11},{9,10},{10,... | collective-permute-start | bytes 196616 | tf_op jit(solution)/shard_map/ppermute | solution.py:420
  26.0 0.0 collective-permute-start.5
  26.1 0.0 copy-start.1
  26.1 0.0 collective-permute-done.6.code_ref
  26.1 1.7 %shard_map.126.refs_6_ = f32[64,64,64]{2,1,0:T(8,128)} custom-call(f32[64,40,128]{2,1,0:T(8,128)S(1)} %bitcast.6, f32[64,24,128]{2,1,0:T(8,128)S(1)} %bitcast.10, s16[24,32,128]{2,1,0:T(8,128)(2,1)S(1)} %collective-permute-done.6.code_ref, f32[64,64,64]{2,1,0:T(8,128)} %shard_map.125.refs_0_), custom_call_target="tpu_custom_call", output_to_operand_aliasing={{}: (3, {})} | custom-call | tf_op jit(solution)/shard_map/pallas_call | solution.py:29
  27.8 0.0 collective-permute-done.3.refs_1_
  27.8 3.7 %collective-permute-done.4.refs_2_ = bf16[64,512]{1,0:T(8,128)(2,1)S(1)} collective-permute-done((bf16[64,512]{1,0:T(8,128)(2,1)S(1)}, bf16[64,512]{1,0:T(8,128)(2,1)S(1)}, u32[]{:S(2)}, u32[]{:S(2)}) %collective-permute-start.4) | collective-permute-done | bytes 65568 | tf_op jit(solution)/shard_map/ppermute | solution.py:420
  31.5 0.0 collective-permute-done.5.refs_3_
  31.5 0.0 collective-permute-done.2.code_ref
  31.5 0.0 copy-done.1
  31.5 2.6 %shard_map.127 = (f32[64,64,64]{2,1,0:T(8,128)}, bf16[64,384]{1,0:T(8,128)(2,1)}) custom-call(f32[64,40,128]{2,1,0:T(8,128)S(1)} %bitcast.7, f32[64,24,128]{2,1,0:T(8,128)S(1)} %bitcast.11, s16[40,32,128]{2,1,0:T(8,128)(2,1)S(1)} %collective-permute-done.2.code_ref, bf16[64,512]{1,0:T(8,128)(2,1)S(1)} %get-tuple-element.28.refs_0_, ...), custom_call_target="tpu_custom_call", output_to_operand_aliasing={{0}: (9, {})} | custom-call | tf_op jit(solution)/shard_map/pallas_call | solution.py:29
  (1 shorter events, 0.0 us)
Async XLA Ops:
  0.6 17.9 %copy-start.2 = (bf16[64,384]{1,0:T(8,128)(2,1)S(1)}, bf16[64,384]{1,0:T(8,128)(2,1)}, u32[]{:S(2)}) copy-start(bf16[64,384]{1,0:T(8,128)(2,1)} %single_ref.1) | copy-start | bytes 147460
  0.6 17.9 %copy-start.4 = (s32[64]{0:T(128)S(1)}, s32[64]{0:T(128)}, u32[]{:S(2)}) copy-start(s32[64]{0:T(128)} %mask_ref.1) | copy-start | bytes 772
  0.7 17.9 %copy-start.3 = (f32[384]{0:T(512)S(1)}, f32[384]{0:T(512)}, u32[]{:S(2)}) copy-start(f32[384]{0:T(512)} %gain_ref.3) | copy-start | bytes 4612
  0.7 17.9 %copy-start = (bf16[384,1536]{1,0:T(8,128)(2,1)S(1)}, bf16[384,1536]{1,0:T(8,128)(2,1)}, u32[]{:S(2)}) copy-start(bf16[384,1536]{1,0:T(8,128)(2,1)} %in_ref.3) | copy-start | bytes 3538948
  5.7 9.3 %collective-permute-start = (s16[40,32,128]{2,1,0:T(8,128)(2,1)S(1)}, s16[40,32,128]{2,1,0:T(8,128)(2,1)S(1)}, u32[]{:S(2)}, u32[]{:S(2)}) collective-permute-start(s16[40,32,128]{2,1,0:T(8,128)(2,1)S(1)} %get-tuple-element.22.refs_0_), channel_id=1, source_target_pairs={{1,4},{3,12},{4,1},{6,9},{9,6},{11,14},{12,3},{14,11},{2,0},{7,5},... | collective-permute-start | bytes 983048 | tf_op jit(solution)/shard_map/ppermute | solution.py:366
  9.2 5.8 %collective-permute-start.1 = (bf16[64,384]{1,0:T(8,128)(2,1)}, bf16[64,384]{1,0:T(8,128)(2,1)S(1)}, u32[]{:S(2)}, u32[]{:S(2)}) collective-permute-start(bf16[64,384]{1,0:T(8,128)(2,1)} %single_ref.1), channel_id=1, source_target_pairs={{2,0},{6,1},{10,2},{14,3},{3,4},{7,5},{11,6},{15,7},{0,8},{4,9},{8... | collective-permute-start | bytes 147464 | tf_op jit(solution)/shard_map/ppermute | solution.py:366
  15.0 16.5 %collective-permute-start.2 = (s16[40,32,128]{2,1,0:T(8,128)(2,1)S(1)}, s16[40,32,128]{2,1,0:T(8,128)(2,1)S(1)}, u32[]{:S(2)}, u32[]{:S(2)}) collective-permute-start(s16[40,32,128]{2,1,0:T(8,128)(2,1)S(1)} %collective-permute-done.code_ref), channel_id=1, source_target_pairs={{0,8},{5,13},{10,2},{15,7},{16,24},{21,29},{26,18},{31,23}} | collective-permute-start | bytes 983048 | tf_op jit(solution)/shard_map/ppermute | solution.py:366
  16.3 9.8 %collective-permute-start.6 = (s16[24,32,128]{2,1,0:T(8,128)(2,1)S(1)}, s16[24,32,128]{2,1,0:T(8,128)(2,1)S(1)}, u32[]{:S(2)}, u32[]{:S(2)}) collective-permute-start(s16[24,32,128]{2,1,0:T(8,128)(2,1)S(1)} %get-tuple-element.25), channel_id=1, source_target_pairs={{0,0},{1,4},{2,8},{3,12},{4,1},{5,5},{6,9},{7,13},{8,2},{9,6},{10,... | collective-permute-start | bytes 589832 | tf_op jit(solution)/shard_map/ppermute | solution.py:366
  20.6 7.2 %collective-permute-start.3 = (bf16[64,512]{1,0:T(8,128)(2,1)S(1)}, bf16[64,512]{1,0:T(8,128)(2,1)S(1)}, u32[]{:S(2)}, u32[]{:S(2)}) collective-permute-start(bf16[64,512]{1,0:T(8,128)(2,1)S(1)} %get-tuple-element.28.refs_0_), channel_id=1, source_target_pairs={{0,2},{1,3},{2,0},{3,1},{4,6},{5,7},{6,4},{7,5},{8,10},{9,11},{10,... | collective-permute-start | bytes 196616 | tf_op jit(solution)/shard_map/ppermute | solution.py:420
  21.3 10.2 %collective-permute-start.4 = (bf16[64,512]{1,0:T(8,128)(2,1)S(1)}, bf16[64,512]{1,0:T(8,128)(2,1)S(1)}, u32[]{:S(2)}, u32[]{:S(2)}) collective-permute-start(bf16[64,512]{1,0:T(8,128)(2,1)S(1)} %get-tuple-element.28.refs_0_), channel_id=1, source_target_pairs={{0,3},{1,2},{2,1},{3,0},{4,7},{5,6},{6,5},{7,4},{8,11},{9,10},{10,... | collective-permute-start | bytes 196616 | tf_op jit(solution)/shard_map/ppermute | solution.py:420
  26.0 5.4 %collective-permute-start.5 = (bf16[64,512]{1,0:T(8,128)(2,1)S(1)}, bf16[64,512]{1,0:T(8,128)(2,1)S(1)}, u32[]{:S(2)}, u32[]{:S(2)}) collective-permute-start(bf16[64,512]{1,0:T(8,128)(2,1)S(1)} %get-tuple-element.28.refs_0_), channel_id=1, source_target_pairs={{0,1},{1,0},{2,3},{3,2},{4,5},{5,4},{6,7},{7,6},{8,9},{9,8},{10,11... | collective-permute-start | bytes 196616 | tf_op jit(solution)/shard_map/ppermute | solution.py:420
  26.1 5.4 %copy-start.1 = (bf16[384,384]{1,0:T(8,128)(2,1)S(1)}, bf16[384,384]{1,0:T(8,128)(2,1)}, u32[]{:S(2)}) copy-start(bf16[384,384]{1,0:T(8,128)(2,1)} %refs_5_.1) | copy-start | bytes 884740

commit v7 on v6

--- a/solution.py
+++ b/solution.py
@@ -185,12 +185,8 @@
     return size // 2
 
 
-def softmax_kernel(part, turn, most, size, heads, first_ref, second_ref, code_ref, *refs):
-    if turn == 2:
-        parts, (gates_ref, weight_ref, _) = refs[:size], refs[size : size + 3]
-        out_ref, single_ref, held, sems, single_held, single_sem = refs[size + 3 :]
-    else:
-        out_ref, held, sems = refs[-3:]
+def softmax_kernel(part, turn, most, size, first_ref, second_ref, code_ref, *refs):
+    out_ref, held, sems = refs[-3:]
     rows, cols, bins = held.shape
     half = cols // 2
     distance = lax.axis_index("col") - lax.axis_index("row")
@@ -242,16 +238,10 @@
         for copy in copies:
             copy.wait()
 
-    if turn == 2:
-        single_held[...] = joined(heads, parts, gates_ref, weight_ref)
-        single_copy = pltpu.make_async_copy(single_held, single_ref, single_sem)
-        single_copy.start()
     if turn == 1:
         work()
     else:
         pl.when(relayed if turn == 2 else jnp.logical_not(relayed))(work)
-    if turn == 2:
-        single_copy.wait()
 
 
 def attention_kernel(
@@ -333,6 +323,14 @@
     return dot(gated, out_weight_ref[...]).astype(jnp.bfloat16)
 
 
+def joined_kernel(heads, count, *refs):
+    parts, (gates_ref, weight_ref, out_ref, held, sem) = refs[:count], refs[count:]
+    held[...] = joined(heads, parts, gates_ref, weight_ref)
+    copy = pltpu.make_async_copy(held, out_ref, sem)
+    copy.start()
+    copy.wait()
+
+
 def partner(place, away, size):
     return place ^ away if size & (size - 1) == 0 else (place + away) % size
 
@@ -421,17 +419,13 @@
     distogram_out = jax.ShapeDtypeStruct((rows, cols, bins), f32)
     single_out = jax.ShapeDtypeStruct((rows, width), bf16)
 
-    def turn(number, part, codes, outs, more=(), scratch=()):
+    def turn(number, part, codes, outs, more=()):
         count = codes[0].shape[0]
         blocks = -(-count // SOFT_STEP)
-        scratch = (
-            pltpu.VMEM((count, cols, bins), f32),
-            pltpu.SemaphoreType.DMA((blocks,)),
-            *scratch,
-        )
+        scratch = (pltpu.VMEM((count, cols, bins), f32), pltpu.SemaphoreType.DMA((blocks,)))
         last = 2 + len(codes) + len(more) - 1
         return call(
-            functools.partial(softmax_kernel, part, number, SOFT_STEP, col_count, heads),
+            functools.partial(softmax_kernel, part, number, SOFT_STEP, col_count),
             outs,
             (*own, *codes, *more),
             scratch=scratch,
@@ -441,12 +435,12 @@
 
     distogram = turn(0, 0, (early, own_code), distogram_out)
     distogram = turn(1, 1, (direct,), distogram_out, (distogram,))
-    distogram, single_update = turn(
-        2,
-        0,
-        (relayed,),
-        (distogram_out, single_out),
-        (*parts, gates, attention_out, distogram),
+    distogram = turn(2, 0, (relayed,), distogram_out, (distogram,))
+    *parts, distogram = lax.optimization_barrier((*parts, distogram))
+    single_update = call(
+        functools.partial(joined_kernel, heads, col_count),
+        single_out,
+        (*parts, gates, attention_out),
         scratch=(pltpu.VMEM((rows, width), bf16), pltpu.SemaphoreType.DMA),
     )
     return (distogram, single_update)

time: 34.3 us -> 34.3 us (level)
  the two profiles are of different devices: /device:TPU:20 before, /device:TPU:0 now
where the time goes in v7:
time: 34.3 us; the launch traced here: 33.9 us
  starting transfers between devices  17.4 us (51%)
  Pallas kernels  14.2 us (41%)
  local copies, waits for them, and re-layouts  0.88 us (3%)
  between operations  0.82 us (2%)
  waiting for transfers between devices  0.5 us (1%)
    pallas_call x7, Pallas kernels, call(): pl.pallas_call(kernel, out_shape=outs, in_specs=[pl.BlockSpec(memory_spac...  14.2 us
    ppermute x4, starting transfers between devices, moved(): return lax.ppermute(value, ('row', 'col'), pairs)  13.1 us
    ppermute x3, starting transfers between devices, body(): parts.append(lax.ppermute(part_sums, 'col', ring))  4.36 us
    unnamed x10, local copies, waits for them, and re-layouts  0.88 us
  transfers between devices with their start and end apart: 7, of which 1 were waited for; matrix products, arithmetic and copies ran while one was open for 0% of the time, Pallas kernels for 24%

profile of v7, /device:TPU:0, one launch (start us, length us, event | category | flops | bytes accessed | tf_op | source)
XLA Modules:
  0.0 33.9 jit_solution(11420056175280178525)
XLA Ops:
  0.6 0.0 copy-start.2
  0.6 0.0 copy-start.4
  0.7 0.0 copy-start.3
  0.7 0.0 copy-start
  0.7 5.0 %shard_map.122 = (f32[2560,128]{1,0:T(8,128)S(1)}, s16[40,32,128]{2,1,0:T(8,128)(2,1)S(1)}, bf16[64,24,128]{2,1,0:T(8,128)(2,1)S(1)}, f32[128]{0:T(128)S(1)}, bf...) custom-call(bf16[64,64,128]{2,1,0:T(8,128)(2,1)} %pair_ref.1, f32[128]{0:T(128)} %gain_ref.2, ...), custom_call_target="tpu_custom_call" | custom-call | tf_op jit(solution)/shard_map/pallas_call | solution.py:29
  5.7 1.3 %collective-permute-start.4 = (s16[40,32,128]{2,1,0:T(8,128)(2,1)S(1)}, s16[40,32,128]{2,1,0:T(8,128)(2,1)S(1)}, u32[]{:S(2)}, u32[]{:S(2)}) collective-permute-start(s16[40,32,128]{2,1,0:T(8,128)(2,1)S(1)} %get-tuple-element.26.refs_0_), channel_id=1, source_target_pairs={{1,4},{3,12},{4,1},{6,9},{9,6},{11,14},{12,3},{14,11},{2,0},{7,5},... | collective-permute-start | bytes 983048 | tf_op jit(solution)/shard_map/ppermute | solution.py:364
  7.0 6.2 %collective-permute-start = (bf16[64,384]{1,0:T(8,128)(2,1)}, bf16[64,384]{1,0:T(8,128)(2,1)S(1)}, u32[]{:S(2)}, u32[]{:S(2)}) collective-permute-start(bf16[64,384]{1,0:T(8,128)(2,1)} %single_ref.1), channel_id=1, source_target_pairs={{2,0},{6,1},{10,2},{14,3},{3,4},{7,5},{11,6},{15,7},{0,8},{4,9},{8... | collective-permute-start | bytes 147464 | tf_op jit(solution)/shard_map/ppermute | solution.py:364
  13.2 2.3 %shard_map.123 = (f32[1536,128]{1,0:T(8,128)S(1)}, s16[24,32,128]{2,1,0:T(8,128)(2,1)S(1)}) custom-call(bf16[64,24,128]{2,1,0:T(8,128)(2,1)S(1)} %get-tuple-element.21.pair_ref, f32[128]{0:T(128)S(1)} %get-tuple-element.22.gain_ref, bf16[128,1024]{1,0:T(8,128)(2,1)S(1)} %get-tuple-element.23.in_ref, bf16[640,256]{1,0:T(8,128)(2,1)S(1)} %get-tuple-element.24.weight_ref), custom_call_target="tpu_custom_call" | custom-call | tf_op jit(solution)/shard_map/pallas_call | solution.py:29
  15.6 0.5 %collective-permute-done.keys_ref = bf16[64,384]{1,0:T(8,128)(2,1)S(1)} collective-permute-done((bf16[64,384]{1,0:T(8,128)(2,1)}, bf16[64,384]{1,0:T(8,128)(2,1)S(1)}, u32[]{:S(2)}, u32[]{:S(2)}) %collective-permute-start) | collective-permute-done | bytes 49184 | tf_op jit(solution)/shard_map/ppermute | solution.py:364
  16.0 0.0 collective-permute-done.4.code_ref
  16.1 4.9 %collective-permute-start.5 = (s16[40,32,128]{2,1,0:T(8,128)(2,1)S(1)}, s16[40,32,128]{2,1,0:T(8,128)(2,1)S(1)}, u32[]{:S(2)}, u32[]{:S(2)}) collective-permute-start(s16[40,32,128]{2,1,0:T(8,128)(2,1)S(1)} %collective-permute-done.4.code_ref), channel_id=1, source_target_pairs={{0,8},{5,13},{10,2},{15,7},{16,24},{21,29},{26,18},{31,23}} | collective-permute-start | bytes 983048 | tf_op jit(solution)/shard_map/ppermute | solution.py:364
  21.0 0.7 %collective-permute-start.6 = (s16[24,32,128]{2,1,0:T(8,128)(2,1)S(1)}, s16[24,32,128]{2,1,0:T(8,128)(2,1)S(1)}, u32[]{:S(2)}, u32[]{:S(2)}) collective-permute-start(s16[24,32,128]{2,1,0:T(8,128)(2,1)S(1)} %get-tuple-element.32), channel_id=1, source_target_pairs={{0,0},{1,4},{2,8},{3,12},{4,1},{5,5},{6,9},{7,13},{8,2},{9,6},{10,... | collective-permute-start | bytes 589832 | tf_op jit(solution)/shard_map/ppermute | solution.py:364
  21.6 0.0 copy-done.2
  21.6 0.0 copy-done.4
  21.7 0.0 copy-done.3
  21.7 0.0 copy-done
  21.7 1.9 %shard_map.124 = (bf16[64,512]{1,0:T(8,128)(2,1)S(1)}, f32[64,384]{1,0:T(8,128)S(1)}) custom-call(bf16[64,384]{1,0:T(8,128)(2,1)S(1)} %copy-done.2, bf16[64,384]{1,0:T(8,128)(2,1)S(1)} %collective-permute-done.keys_ref, s32[64]{0:T(128)S(1)} %copy-done.4, f32[384]{0:T(512)S(1)} %copy-done.3, bf16[384,1536]{1,0:T(8,128)(2,1)S(1)} %copy-done, ...), custom_call_target="tpu_custom_call" | custom-call | tf_op jit(solution)/shard_map/pallas_call | solution.py:29
  23.6 2.1 %collective-permute-start.1 = (bf16[64,512]{1,0:T(8,128)(2,1)S(1)}, bf16[64,512]{1,0:T(8,128)(2,1)S(1)}, u32[]{:S(2)}, u32[]{:S(2)}) collective-permute-start(bf16[64,512]{1,0:T(8,128)(2,1)S(1)} %get-tuple-element.35.refs_0_), channel_id=1, source_target_pairs={{0,2},{1,3},{2,0},{3,1},{4,6},{5,7},{6,4},{7,5},{8,10},{9,11},{10,... | collective-permute-start | bytes 196616 | tf_op jit(solution)/shard_map/ppermute | solution.py:418
  25.8 2.2 %collective-permute-start.2 = (bf16[64,512]{1,0:T(8,128)(2,1)S(1)}, bf16[64,512]{1,0:T(8,128)(2,1)S(1)}, u32[]{:S(2)}, u32[]{:S(2)}) collective-permute-start(bf16[64,512]{1,0:T(8,128)(2,1)S(1)} %get-tuple-element.35.refs_0_), channel_id=1, source_target_pairs={{0,3},{1,2},{2,1},{3,0},{4,7},{5,6},{6,5},{7,4},{8,11},{9,10},{10,... | collective-permute-start | bytes 196616 | tf_op jit(solution)/shard_map/ppermute | solution.py:418
  27.9 0.0 collective-permute-start.3
  28.0 2.2 %shard_map.125.refs_0_ = f32[64,64,64]{2,1,0:T(8,128)} custom-call(f32[64,40,128]{2,1,0:T(8,128)S(1)} %bitcast.5, f32[64,24,128]{2,1,0:T(8,128)S(1)} %bitcast.9, s16[40,32,128]{2,1,0:T(8,128)(2,1)S(1)} %collective-permute-done.4.code_ref, s16[40,32,128]{2,1,0:T(8,128)(2,1)S(1)} %get-tuple-element.26.refs_0_), custom_call_target="tpu_custom_call" | custom-call | tf_op jit(solution)/shard_map/pallas_call | solution.py:29
  30.2 0.0 collective-permute-done.6.code_ref
  30.2 1.7 %shard_map.126.refs_0_ = f32[64,64,64]{2,1,0:T(8,128)} custom-call(f32[64,40,128]{2,1,0:T(8,128)S(1)} %bitcast.6, f32[64,24,128]{2,1,0:T(8,128)S(1)} %bitcast.10, s16[24,32,128]{2,1,0:T(8,128)(2,1)S(1)} %collective-permute-done.6.code_ref, f32[64,64,64]{2,1,0:T(8,128)} %shard_map.125.refs_0_), custom_call_target="tpu_custom_call", output_to_operand_aliasing={{}: (3, {})} | custom-call | tf_op jit(solution)/shard_map/pallas_call | solution.py:29
  31.8 0.0 copy-start.1
  31.9 0.0 collective-permute-done.5.code_ref
  31.9 0.0 collective-permute-done.1.refs_1_
  31.9 0.0 collective-permute-done.2.refs_2_
  31.9 0.0 collective-permute-done.3.refs_3_
  32.0 0.9 %copy-done.1 = bf16[384,384]{1,0:T(8,128)(2,1)S(1)} copy-done((bf16[384,384]{1,0:T(8,128)(2,1)S(1)}, bf16[384,384]{1,0:T(8,128)(2,1)}, u32[]{:S(2)}) %copy-start.1) | copy-done | bytes 294936
  32.8 1.0 %shard_map.128 = bf16[64,384]{1,0:T(8,128)(2,1)} custom-call(bf16[64,512]{1,0:T(8,128)(2,1)S(1)} %get-tuple-element.35.refs_0_, bf16[64,512]{1,0:T(8,128)(2,1)S(1)} %collective-permute-done.1.refs_1_, bf16[64,512]{1,0:T(8,128)(2,1)S(1)} %collective-permute-done.2.refs_2_, bf16[64,512]{1,0:T(8,128)(2,1)S(1)} %collective-permute-done.3.refs_3_, ...), custom_call_target="tpu_custom_call" | custom-call | tf_op jit(solution)/shard_map/pallas_call | solution.py:29
  (1 shorter events, 0.0 us)
Async XLA Ops:
  0.6 21.0 %copy-start.2 = (bf16[64,384]{1,0:T(8,128)(2,1)S(1)}, bf16[64,384]{1,0:T(8,128)(2,1)}, u32[]{:S(2)}) copy-start(bf16[64,384]{1,0:T(8,128)(2,1)} %single_ref.1) | copy-start | bytes 147460
  0.6 21.0 %copy-start.4 = (s32[64]{0:T(128)S(1)}, s32[64]{0:T(128)}, u32[]{:S(2)}) copy-start(s32[64]{0:T(128)} %mask_ref.1) | copy-start | bytes 772
  0.7 21.0 %copy-start.3 = (f32[384]{0:T(512)S(1)}, f32[384]{0:T(512)}, u32[]{:S(2)}) copy-start(f32[384]{0:T(512)} %gain_ref.3) | copy-start | bytes 4612
  0.7 21.0 %copy-start = (bf16[384,1536]{1,0:T(8,128)(2,1)S(1)}, bf16[384,1536]{1,0:T(8,128)(2,1)}, u32[]{:S(2)}) copy-start(bf16[384,1536]{1,0:T(8,128)(2,1)} %in_ref.3) | copy-start | bytes 3538948
  5.7 10.3 %collective-permute-start.4 = (s16[40,32,128]{2,1,0:T(8,128)(2,1)S(1)}, s16[40,32,128]{2,1,0:T(8,128)(2,1)S(1)}, u32[]{:S(2)}, u32[]{:S(2)}) collective-permute-start(s16[40,32,128]{2,1,0:T(8,128)(2,1)S(1)} %get-tuple-element.26.refs_0_), channel_id=1, source_target_pairs={{1,4},{3,12},{4,1},{6,9},{9,6},{11,14},{12,3},{14,11},{2,0},{7,5},... | collective-permute-start | bytes 983048 | tf_op jit(solution)/shard_map/ppermute | solution.py:364
  7.0 9.0 %collective-permute-start = (bf16[64,384]{1,0:T(8,128)(2,1)}, bf16[64,384]{1,0:T(8,128)(2,1)S(1)}, u32[]{:S(2)}, u32[]{:S(2)}) collective-permute-start(bf16[64,384]{1,0:T(8,128)(2,1)} %single_ref.1), channel_id=1, source_target_pairs={{2,0},{6,1},{10,2},{14,3},{3,4},{7,5},{11,6},{15,7},{0,8},{4,9},{8... | collective-permute-start | bytes 147464 | tf_op jit(solution)/shard_map/ppermute | solution.py:364
  16.1 15.8 %collective-permute-start.5 = (s16[40,32,128]{2,1,0:T(8,128)(2,1)S(1)}, s16[40,32,128]{2,1,0:T(8,128)(2,1)S(1)}, u32[]{:S(2)}, u32[]{:S(2)}) collective-permute-start(s16[40,32,128]{2,1,0:T(8,128)(2,1)S(1)} %collective-permute-done.4.code_ref), channel_id=1, source_target_pairs={{0,8},{5,13},{10,2},{15,7},{16,24},{21,29},{26,18},{31,23}} | collective-permute-start | bytes 983048 | tf_op jit(solution)/shard_map/ppermute | solution.py:364
  21.0 9.2 %collective-permute-start.6 = (s16[24,32,128]{2,1,0:T(8,128)(2,1)S(1)}, s16[24,32,128]{2,1,0:T(8,128)(2,1)S(1)}, u32[]{:S(2)}, u32[]{:S(2)}) collective-permute-start(s16[24,32,128]{2,1,0:T(8,128)(2,1)S(1)} %get-tuple-element.32), channel_id=1, source_target_pairs={{0,0},{1,4},{2,8},{3,12},{4,1},{5,5},{6,9},{7,13},{8,2},{9,6},{10,... | collective-permute-start | bytes 589832 | tf_op jit(solution)/shard_map/ppermute | solution.py:364
  23.6 8.3 %collective-permute-start.1 = (bf16[64,512]{1,0:T(8,128)(2,1)S(1)}, bf16[64,512]{1,0:T(8,128)(2,1)S(1)}, u32[]{:S(2)}, u32[]{:S(2)}) collective-permute-start(bf16[64,512]{1,0:T(8,128)(2,1)S(1)} %get-tuple-element.35.refs_0_), channel_id=1, source_target_pairs={{0,2},{1,3},{2,0},{3,1},{4,6},{5,7},{6,4},{7,5},{8,10},{9,11},{10,... | collective-permute-start | bytes 196616 | tf_op jit(solution)/shard_map/ppermute | solution.py:418
  25.8 6.2 %collective-permute-start.2 = (bf16[64,512]{1,0:T(8,128)(2,1)S(1)}, bf16[64,512]{1,0:T(8,128)(2,1)S(1)}, u32[]{:S(2)}, u32[]{:S(2)}) collective-permute-start(bf16[64,512]{1,0:T(8,128)(2,1)S(1)} %get-tuple-element.35.refs_0_), channel_id=1, source_target_pairs={{0,3},{1,2},{2,1},{3,0},{4,7},{5,6},{6,5},{7,4},{8,11},{9,10},{10,... | collective-permute-start | bytes 196616 | tf_op jit(solution)/shard_map/ppermute | solution.py:418
  27.9 4.0 %collective-permute-start.3 = (bf16[64,512]{1,0:T(8,128)(2,1)S(1)}, bf16[64,512]{1,0:T(8,128)(2,1)S(1)}, u32[]{:S(2)}, u32[]{:S(2)}) collective-permute-start(bf16[64,512]{1,0:T(8,128)(2,1)S(1)} %get-tuple-element.35.refs_0_), channel_id=1, source_target_pairs={{0,1},{1,0},{2,3},{3,2},{4,5},{5,4},{6,7},{7,6},{8,9},{9,8},{10,11... | collective-permute-start | bytes 196616 | tf_op jit(solution)/shard_map/ppermute | solution.py:418
  31.8 1.0 %copy-start.1 = (bf16[384,384]{1,0:T(8,128)(2,1)S(1)}, bf16[384,384]{1,0:T(8,128)(2,1)}, u32[]{:S(2)}) copy-start(bf16[384,384]{1,0:T(8,128)(2,1)} %refs_5_.1) | copy-start | bytes 884740
